TPU v7x, 512 devices: a whole 4x8x8 slice. The times are simulated.
512 devices in a mesh: pts: 128 (over y, z, core), grp: 4 (over x).
Axes of the slice: x: 4, y: 8, z: 8, core: 2. Of those that a mesh axis runs over, the one named last changes fastest.
Arguments:
- jacobian: bfloat16 [512, 6, 128, 3, 256], P(('pts', 'grp')), may hold values from -0.21875 to 0.21875
- point_blocks: float32 [512, 6, 256], P(('pts', 'grp')), may hold values from -0.5 to 4, as said below
- point_grad: bfloat16 [512, 3, 256], P(('pts', 'grp')), may hold values from -6 to 6
- camera_grad: float32 [512, 128], P(('pts', 'grp')), may hold values from -6 to 6
- damping: float32 [512, 128], replicated, may hold values from 1 to 8
- incidence: int32 [512, 6], P(('pts', 'grp')), may hold values from 0 to 511, as said below
- tile_owner: int32 [128], replicated, may hold values from 0 to 127, each once
- front_first: int32 [1], replicated, may hold values from 0 to 511
Outputs:
- tiles_out: float32 [4096, 128, 128], P(('pts', 'grp'))
- rhs_out: float32 [512, 128], P(('pts', 'grp'))
- front_panel: float32 [2304, 512], P(None, 'grp')
Inputs may be any that keep to these rules, and one draw needn't show every extreme that they name: `incidence`: point cluster p names 6 different camera clusters, all among (p + t) mod 512 for t from 0 to 7. `point_blocks`: each point's diagonal entries exceed the sum of the magnitudes of the two off-diagonal entries of their row by 0.1 or more. `tile_owner`: A permutation of the pts indices.
All inputs are finite; a program needn't handle non-finite values.
Results may differ from a plain program's by a relative error of at most 0.0022.
Values sent between devices are 32-bit elements; how exact they have to be, the bound alone decides.
A program may use at most 128 MiB of HBM per device.

v0:
```python
import jax
import jax.numpy as jnp
import numpy as np
from jax import lax
from jax.sharding import PartitionSpec as P

TOUCH = 6
BAND = 8
FRONT = 4


PRECISE = lax.Precision.HIGHEST


def shifted(value, axis, steps):
    count = lax.axis_size(axis)
    pairs = [(source, (source + steps) % count) for source in range(count)]
    return lax.ppermute(value, axis, pairs)


def invert_blocks(blocks):
    diag_x = blocks[:, 0]
    diag_y = blocks[:, 1]
    diag_z = blocks[:, 2]
    cross_xy = blocks[:, 3]
    cross_xz = blocks[:, 4]
    cross_yz = blocks[:, 5]
    adj_xx = diag_y * diag_z - cross_yz * cross_yz
    adj_yy = diag_x * diag_z - cross_xz * cross_xz
    adj_zz = diag_x * diag_y - cross_xy * cross_xy
    adj_xy = cross_xz * cross_yz - cross_xy * diag_z
    adj_xz = cross_xy * cross_yz - diag_y * cross_xz
    adj_yz = cross_xy * cross_xz - diag_x * cross_yz
    determinant = diag_x * adj_xx + cross_xy * adj_xy + cross_xz * adj_xz
    inverse_det = 1.0 / determinant
    return [
        [adj_xx * inverse_det, adj_xy * inverse_det, adj_xz * inverse_det],
        [adj_xy * inverse_det, adj_yy * inverse_det, adj_yz * inverse_det],
        [adj_xz * inverse_det, adj_yz * inverse_det, adj_zz * inverse_det],
    ]


def scale_jacobian(jacobian, blocks):
    inverse = invert_blocks(blocks)
    widened = jacobian.astype(jnp.float32)
    columns = []
    for target in range(3):
        summed = widened[:, :, :, 0, :] * inverse[0][target][:, None, None, :]
        summed = summed + widened[:, :, :, 1, :] * inverse[1][target][:, None, None, :]
        summed = summed + widened[:, :, :, 2, :] * inverse[2][target][:, None, None, :]
        columns.append(summed)
    return jnp.stack(columns, axis=3).astype(jnp.bfloat16)


def band_table(reach_rows, reach_sum):
    row_list = []
    offset_list = []
    for row_pos in range(reach_rows):
        for offset in range(BAND):
            if row_pos + offset <= reach_sum:
                row_list.append(row_pos)
                offset_list.append(offset)
    return (np.array(row_list), np.array(offset_list))


def route_rows(tiles, tile_owner, base, row_list, offset_list, pts_count):
    offsets = BAND * row_list + offset_list
    capacity = int(offsets.max()) // pts_count + 1
    residue = jnp.mod(base + jnp.asarray(offsets), pts_count)
    target = tile_owner[residue] * capacity + jnp.asarray(offsets // pts_count)
    sending = (jnp.arange(pts_count * capacity)[:, None] == target[None, :]).astype(jnp.float32)
    return (jnp.einsum("dt,trc->drc", sending, tiles, precision=PRECISE), capacity)


def collect_rows(
    incoming, capacity, perm_inverse, anchors, usable_test, clusters, grp_count, pts_count
):
    sender = jnp.arange(pts_count * capacity) // capacity
    slot_of = jnp.arange(pts_count * capacity) % capacity
    sender_anchor = anchors(sender)
    arrived = jnp.mod(perm_inverse - BAND * sender_anchor, pts_count) + slot_of * pts_count
    row_pos = arrived // BAND
    offset = arrived % BAND
    usable = usable_test(row_pos, offset)
    home_row = jnp.mod(sender_anchor + row_pos, clusters)
    owner_slot = (BAND * home_row + offset) // pts_count
    gathering = (
        (jnp.arange(BAND * grp_count)[:, None] == owner_slot[None, :]) & usable[None, :]
    ).astype(jnp.float32)
    return jnp.einsum("ms,src->mrc", gathering, incoming, precision=PRECISE)


def per_device(
    jacobian, point_blocks, point_grad, camera_grad, damping, incidence, tile_owner, front_first
):
    pts_count = lax.axis_size("pts")
    grp_count = lax.axis_size("grp")
    clusters = pts_count * grp_count
    my_grp = lax.axis_index("grp")
    my_pts = lax.axis_index("pts")
    device = my_pts * grp_count + my_grp
    local_count = jacobian.shape[0]
    cam_rows = jacobian.shape[2]
    point_cols = 3 * jacobian.shape[4]
    window_len = 2 * BAND - 2 + FRONT
    reach = 2 * BAND - 1
    scaled = scale_jacobian(jacobian, point_blocks).reshape(
        local_count, TOUCH, cam_rows, point_cols
    )
    jac_flat = jacobian.reshape(local_count, TOUCH, cam_rows, point_cols)
    local_slot = jnp.mod(incidence - device, clusters)
    placing = (local_slot[:, None, :] == jnp.arange(BAND)[None, :, None]).astype(jnp.bfloat16)
    placed_scaled = jnp.einsum(
        "ptk,pkrx->ptrx", placing, scaled, preferred_element_type=jnp.float32
    ).astype(jnp.bfloat16)
    placed_jac = jnp.einsum(
        "ptk,pkrx->ptrx", placing, jac_flat, preferred_element_type=jnp.float32
    ).astype(jnp.bfloat16)
    band_grid = jnp.einsum(
        "ptrx,pqcx->tqrc", placed_scaled, placed_jac, preferred_element_type=jnp.float32
    )
    band_rhs = jnp.einsum(
        "ptrx,px->tr",
        placed_scaled,
        point_grad.reshape(local_count, point_cols),
        preferred_element_type=jnp.float32,
    )
    perm_inverse = jnp.sum(jnp.arange(pts_count) * (tile_owner == my_pts))
    row_list, offset_list = band_table(BAND, BAND - 1)
    band_tiles = band_grid[row_list, row_list + offset_list]
    quarters = lax.all_to_all(band_tiles, "grp", split_axis=1, concat_axis=0, tiled=True)
    reach_union = BAND + grp_count - 2
    union_rows_list, union_offsets = band_table(reach_union + 1, reach_union)
    lookup = {}
    for position in range(len(union_rows_list)):
        lookup[int(union_rows_list[position]), int(union_offsets[position])] = position
    merge_table = np.zeros((len(union_rows_list), grp_count * len(row_list)), np.float32)
    for source_grp in range(grp_count):
        for position in range(len(row_list)):
            merge_table[
                lookup[source_grp + int(row_list[position]), int(offset_list[position])],
                source_grp * len(row_list) + position,
            ] = 1.0
    union_rows = jnp.einsum("us,src->urc", jnp.asarray(merge_table), quarters, precision=PRECISE)
    outgoing, capacity = route_rows(
        union_rows, tile_owner, BAND * grp_count * my_pts, union_rows_list, union_offsets, pts_count
    )
    incoming = lax.all_to_all(outgoing, "pts", split_axis=0, concat_axis=0, tiled=True)
    owner_rows = collect_rows(
        incoming,
        capacity,
        perm_inverse,
        lambda sender: sender * grp_count,
        lambda row_pos, offset: row_pos + offset <= reach_union,
        clusters,
        grp_count,
        pts_count,
    )
    owned = lax.all_to_all(owner_rows, "grp", split_axis=0, concat_axis=1, tiled=True)
    tile_id = perm_inverse + pts_count * (BAND * my_grp + jnp.arange(BAND))
    home_row = tile_id // BAND
    offset = tile_id % BAND
    other_row = jnp.mod(home_row + offset, clusters)
    pick_damp = (home_row[:, None] == jnp.arange(clusters)[None, :]).astype(jnp.float32)
    damp_rows = jnp.dot(pick_damp, damping, precision=PRECISE)
    identity = jnp.eye(cam_rows, dtype=jnp.float32)
    owned = owned + jnp.where(
        (offset == 0)[:, None, None], damp_rows[:, :, None] * identity[None, :, :], 0.0
    )
    summed = band_rhs[0]
    for step in range(1, BAND):
        summed = summed + shifted(band_rhs[step], ("pts", "grp"), step)
    reduced = camera_grad - summed[None, :]
    front_start = front_first[0]
    window_base = front_start - (BAND - 1)
    pos_home = jnp.mod(home_row - window_base, clusters)
    pos_other = jnp.mod(other_row - window_base, clusters)
    front_axis = jnp.arange(FRONT)[:, None, None]
    reach_axis = jnp.arange(reach)[None, :, None]
    direct = (
        (pos_other[None, None, :] == BAND - 1 + front_axis)
        & (pos_home[None, None, :] == front_axis + reach_axis)
    ).astype(jnp.float32)
    mirror = (
        (pos_home[None, None, :] == BAND - 1 + front_axis)
        & (offset[None, None, :] > 0)
        & (pos_other[None, None, :] == front_axis + reach_axis)
    ).astype(jnp.float32)
    front_rows = jnp.einsum("kes,sab->keab", direct, owned, precision=PRECISE) + jnp.einsum(
        "kes,sba->keab", mirror, owned, precision=PRECISE
    )
    my_pos = jnp.mod(device - window_base, clusters)
    window_rhs = (jnp.arange(window_len)[:, None] == my_pos).astype(jnp.float32) * reduced
    front_rows, window_rhs = lax.psum((front_rows, window_rhs), ("pts", "grp"))
    flat_rows = jnp.concatenate(
        [
            front_rows.reshape(FRONT * reach, cam_rows, cam_rows),
            jnp.zeros((1, cam_rows, cam_rows), jnp.float32),
        ],
        axis=0,
    )
    lookup_table = np.full((window_len, FRONT), FRONT * reach, np.int32)
    for position in range(window_len):
        for front_pos in range(FRONT):
            if 0 <= position - front_pos < reach:
                lookup_table[position, front_pos] = front_pos * reach + position - front_pos
    columns = (
        flat_rows[lookup_table]
        .transpose(0, 2, 1, 3)
        .reshape(window_len * cam_rows, FRONT * cam_rows)
    )
    square = columns[(BAND - 1) * cam_rows : (BAND - 1 + FRONT) * cam_rows]
    factor = jnp.linalg.cholesky(square)
    panel = jax.scipy.linalg.solve_triangular(factor, columns.T, lower=True).T
    share = FRONT * cam_rows // grp_count
    front_panel = lax.dynamic_slice_in_dim(panel, my_grp * share, share, 1)
    panel_blocks = panel.reshape(window_len, cam_rows, FRONT * cam_rows)

    def inside_rest(position):
        return (position < window_len) & ((position < BAND - 1) | (position >= BAND - 1 + FRONT))

    update_mask = inside_rest(pos_home) & inside_rest(pos_other)
    pick_home = (pos_home[:, None] == jnp.arange(window_len)[None, :]).astype(jnp.float32)
    pick_other = (pos_other[:, None] == jnp.arange(window_len)[None, :]).astype(jnp.float32)
    rows_home = jnp.einsum("sp,pra->sra", pick_home, panel_blocks, precision=PRECISE)
    rows_other = jnp.einsum("sp,pra->sra", pick_other, panel_blocks, precision=PRECISE)
    change = jnp.einsum("sra,sca->src", rows_home, rows_other, precision=PRECISE)
    tiles_out = owned - jnp.where(update_mask[:, None, None], change, 0.0)
    solved_front = jax.scipy.linalg.solve_triangular(
        factor, window_rhs[BAND - 1 : BAND - 1 + FRONT].reshape(FRONT * cam_rows), lower=True
    )
    my_row = lax.dynamic_index_in_dim(
        panel_blocks, jnp.clip(my_pos, 0, window_len - 1), 0, keepdims=False
    )
    correction = reduced[0] - jnp.dot(my_row, solved_front, precision=PRECISE)
    front_piece = lax.dynamic_index_in_dim(
        solved_front.reshape(FRONT, cam_rows),
        jnp.clip(my_pos - (BAND - 1), 0, FRONT - 1),
        0,
        keepdims=False,
    )
    in_front = (my_pos >= BAND - 1) & (my_pos < BAND - 1 + FRONT)
    in_window = my_pos < window_len
    rhs_out = jnp.where(in_front, front_piece, jnp.where(in_window, correction, reduced[0]))[
        None, :
    ]
    return (tiles_out, rhs_out, front_panel)


def solution(mesh):
    in_specs = (
        P(("pts", "grp"), None, None, None, None),
        P(("pts", "grp"), None, None),
        P(("pts", "grp"), None, None),
        P(("pts", "grp"), None),
        P(),
        P(("pts", "grp"), None),
        P(),
        P(),
    )
    out_specs = (P(("pts", "grp"), None, None), P(("pts", "grp"), None), P(None, "grp"))
    return jax.shard_map(
        per_device, mesh=mesh, in_specs=in_specs, out_specs=out_specs, check_vma=False
    )
```

profile of v0, /device:TPU:1, one launch (start us, length us, event | category | flops | bytes accessed | tf_op | source)
XLA Modules:
  0.0 661.8 jit_solution(12736394999096253480)
XLA Ops:
  11.8 2.1 copy.46
  18.5 3.5 convolution_bitcast_fusion
  21.9 2.9 gather_fusion.1
  24.9 2.2 copy.49
  27.0 5.0 all-to-all-start
  32.8 25.5 %all-to-all-done = f32[36,128,128]{2,0,1:T(8,128)S(1)} async-done(((f32[36,128,128]{2,0,1:T(8,128)}), f32[36,128,128]{2,0,1:T(8,128)S(1)}, u32[]{:S(2)}, u32[]{:S(2)}) %all-to-all-start) | async-done | bytes 2359328 | tf_op jit(solution)/shard_map/all_to_all | solution.py:131
  58.8 2.7 fusion.12
  62.6 2.6 copy.52
  65.2 24.2 %all-to-all-start.1 = ((f32[128,32,128]{2,1,0:T(8,128)}), f32[128,32,128]{2,1,0:T(8,128)S(1)}, u32[]{:S(2)}, u32[]{:S(2)}) async-start(f32[128,32,128]{2,1,0:T(8,128)} %copy.52), calls=%async_computation.1 | async-start | bytes 4194304 | tf_op jit(solution)/shard_map/all_to_all | solution.py:148
  92.8 50.2 %all-to-all-done.1 = f32[128,32,128]{2,1,0:T(8,128)S(1)} async-done(((f32[128,32,128]{2,1,0:T(8,128)}), f32[128,32,128]{2,1,0:T(8,128)S(1)}, u32[]{:S(2)}, u32[]{:S(2)}) %all-to-all-start.1) | async-done | bytes 2097184 | tf_op jit(solution)/shard_map/all_to_all | solution.py:148
  143.0 2.0 fusion.17
  146.1 3.5 all-to-all-start.2
  150.5 5.9 all-to-all-done.2
  157.0 1.9 fusion.47
  158.9 2.0 bitcast_add_fusion
  160.9 3.1 copy.58
  165.4 3.5 fusion.143
  169.0 2.2 collective-permute-start
  171.3 3.7 collective-permute-start.1
  175.0 6.8 %collective-permute-start.2 = (f32[128]{0:T(128)S(1)}, f32[128]{0:T(128)S(1)}, u32[]{:S(2)}, u32[]{:S(2)}) collective-permute-start(f32[128]{0:T(128)S(1)} %get-tuple-element.62), channel_id=1, source_target_pairs={{0,3},{1,4},{2,5},{3,6},{4,7},{5,8},{6,9},{7,10},{8,11},{9,12},{10... | collective-permute-start | bytes 1544 | tf_op jit(solution)/shard_map/ppermute | solution.py:18
  181.9 2.2 collective-permute-start.3
  184.1 4.7 collective-permute-start.4
  188.9 4.3 collective-permute-start.5
  193.2 4.0 collective-permute-start.6
  198.9 2.8 collective-permute-done.6
  201.8 96.6 %psum.15 = f32[18,128]{1,0:T(8,128)S(1)} all-reduce(f32[18,128]{1,0:T(8,128)S(1)} %broadcast_multiply_fusion), channel_id=1, replica_groups=mesh['pts'=128,'grp'=4] {'pts','grp'}, use_global_device_ids=true, to_apply=%region_10.11 | all-reduce | flops 2304 | bytes 18432 | tf_op jit(solution)/shard_map/psum | solution.py:194
  298.4 147.7 %all-reduce.4.cloned.1.call-done = f32[60,128,128]{2,1,0:T(8,128)} async-done(((f32[60,128,128]{2,1,0:T(8,128)}), f32[60,128,128]{2,1,0:T(8,128)}) %all-reduce.4.cloned.1.call-update) | async-done | bytes 3932176 | tf_op jit(solution)/shard_map/psum | solution.py:194
  446.1 4.5 concatenate.34
  450.6 5.2 gather_fusion.2
  461.3 11.7 %cholesky.86 = f32[128,128]{1,0:T(8,128)S(1)} custom-call(f32[128,128]{1,0:T(8,128)S(1)} %cholesky.232), custom_call_target="Cholesky" | custom-call | tf_op jit(solution)/shard_map/jit(cholesky)/cholesky | solution.py:213
  473.2 6.7 %copy.75 = f32[18,128,4,128]{1,0,3,2:T(8,128)} copy(f32[18,128,4,128]{3,1,2,0:T(8,128)} %bitcast.261) | data formatting | bytes 9437184 | tf_op jit(solution)/shard_map/reshape | solution.py:210
  479.9 9.8 %custom-call.34 = f32[1,128,128]{1,2,0:T(8,128)S(1)} custom-call(f32[1,128,128]{2,1,0:T(8,128)S(1)} %get-tuple-element.50), custom_call_target="InvertDiagBlocksLowerTriangular" | custom-call | tf_op jit(solution)/shard_map/jit(cholesky)/cholesky | solution.py:213
  490.4 11.7 %cholesky.183 = f32[128,128]{1,0:T(8,128)S(1)} custom-call(f32[128,128]{1,0:T(8,128)S(1)} %cholesky.236), custom_call_target="Cholesky" | custom-call | tf_op jit(solution)/shard_map/jit(cholesky)/cholesky | solution.py:213
  503.5 9.8 %custom-call.35 = f32[1,128,128]{1,2,0:T(8,128)S(1)} custom-call(f32[1,128,128]{2,1,0:T(8,128)S(1)} %get-tuple-element.47), custom_call_target="InvertDiagBlocksLowerTriangular" | custom-call | tf_op jit(solution)/shard_map/jit(cholesky)/cholesky | solution.py:213
  513.9 11.9 %cholesky.204 = f32[128,128]{1,0:T(8,128)S(1)} custom-call(f32[128,128]{1,0:T(8,128)S(1)} %cholesky.241), custom_call_target="Cholesky" | custom-call | tf_op jit(solution)/shard_map/jit(cholesky)/cholesky | solution.py:213
  526.5 9.8 %custom-call.36 = f32[1,128,128]{1,2,0:T(8,128)S(1)} custom-call(f32[1,128,128]{2,1,0:T(8,128)S(1)} %get-tuple-element.44), custom_call_target="InvertDiagBlocksLowerTriangular" | custom-call | tf_op jit(solution)/shard_map/jit(cholesky)/cholesky | solution.py:213
  536.9 11.7 %cholesky.221 = f32[128,128]{1,0:T(8,128)S(1)} custom-call(f32[128,128]{1,0:T(8,128)S(1)} %convolution_subtract_fusion.5), custom_call_target="Cholesky" | custom-call | tf_op jit(solution)/shard_map/jit(cholesky)/cholesky | solution.py:213
  552.1 8.0 %while.1 = (s32[]{:T(128)}, f32[512,512]{1,0:T(8,128)S(1)}, s32[4,2]{0,1:T(2,128)S(1)}, f32[4,128,128]{2,1,0:T(8,128)S(1)}, s32[]{:T(128)}) while((s32[]{:T(128)}, f32[512,512]{1,0:T(8,128)S(1)}, s32[4,2]{0,1:T(2,128)S(1)}, f32[4,128,128]{2,1,0:T(8,128)S(1)}, s32[]{:T(128)}) %tuple.57), condition=%wide.while_cond, body=%wide.while_body.sunk | while | flops 2 | bytes 131181 | solution.py:214
  560.1 39.5 %custom-call.37 = f32[4,128,128]{1,2,0:T(8,128)S(1)} custom-call(f32[4,128,128]{2,1,0:T(8,128)S(1)} %get-tuple-element.10), custom_call_target="InvertDiagBlocksLowerTriangular" | custom-call | tf_op jit(solution)/shard_map/jit(_solve_triangular)/triangular_solve | solution.py:214
  599.6 3.8 copy.113
  609.5 2.2 convolution_subtract_fusion.1
  612.8 4.2 pad_maximum_fusion
  617.1 6.0 copy.63
  623.1 7.7 %fusion.2 = f32[8,128,512]{2,0,1:T(8,128)S(1)} fusion(f32[18,128,512]{2,1,0:T(8,128)} %bitcast.256, s32[8]{0:T(128)S(1)} %get-tuple-element.30), kind=kOutput, calls=%fused_computation.7 | convolution fusion | flops 113246352 | bytes 6815776 | tf_op jit(solution)/shard_map/sp,pra->sra/dot_general | solution.py:225
  630.9 5.9 fusion
  640.9 2.4 dynamic-slice_bitcast_fusion
  643.3 2.7 copy.68
  646.0 6.8 %fusion.28 = f32[8,128,128]{2,1,0:T(8,128)} fusion(f32[8,128,128]{2,1,0:T(8,128)S(1)} %bitcast_add_fusion.2, f32[8,128,512]{2,0,1:T(8,128)} %fusion, f32[8,128,512]{2,0,1:T(8,128)S(1)} %fusion.2, pred[8]{0:T(512)(128)(4,1)S(1)} %get-tuple-element.28), kind=kOutput, calls=%fused_computation.38 | convolution fusion | flops 805568512 | bytes 5242888 | tf_op jit(solution)/shard_map/sra,sca->src/dot_general | solution.py:227
  (133 shorter events, 51.4 us)
Async XLA Ops:
  7.2 143.1 %copy-start = (f32[512,128]{1,0:T(8,128)S(1)}, f32[512,128]{1,0:T(8,128)}, u32[]{:S(2)}) copy-start(f32[512,128]{1,0:T(8,128)} %param.21) | copy-start | bytes 786436
  11.8 4.0 copy-start.15
  15.8 1.4 copy-start.6
  17.2 1.2 copy-start.4
  18.5 3.5 copy-start.10
  27.0 5.0 copy-start.16
  27.0 5.0 copy-start.2
  27.0 31.3 %all-to-all-start = ((f32[36,128,128]{2,0,1:T(8,128)}), f32[36,128,128]{2,0,1:T(8,128)S(1)}, u32[]{:S(2)}, u32[]{:S(2)}) async-start(f32[36,128,128]{2,0,1:T(8,128)} %copy.49), calls=%async_computation | async-start | bytes 5242880 | tf_op jit(solution)/shard_map/all_to_all | solution.py:131
  32.8 26.0 %copy-start.11 = (f32[60,144,1]{1,0,2:T(8,128)S(1)}, f32[60,144,1]{1,0,2:T(8,128)}, u32[]{:S(2)}) copy-start(f32[60,144,1]{1,0,2:T(8,128)} %constant.440) | copy-start | bytes 103684
  65.2 77.8 %all-to-all-start.1 = ((f32[128,32,128]{2,1,0:T(8,128)}), f32[128,32,128]{2,1,0:T(8,128)S(1)}, u32[]{:S(2)}, u32[]{:S(2)}) async-start(f32[128,32,128]{2,1,0:T(8,128)} %copy.52), calls=%async_computation.1 | async-start | bytes 4194304 | tf_op jit(solution)/shard_map/all_to_all | solution.py:148
  146.1 10.4 %all-to-all-start.2 = ((f32[32,32,128]{2,1,0:T(8,128)}), f32[32,32,128]{2,1,0:T(8,128)S(1)}, u32[]{:S(2)}, u32[]{:S(2)}) async-start(f32[32,32,128]{2,1,0:T(8,128)} %copy.54), calls=%async_computation.2 | async-start | bytes 1048576 | tf_op jit(solution)/shard_map/all_to_all | solution.py:159
  149.6 296.5 %all-reduce.4.cloned.1.call-start = ((), (), s32[]{:S(2)}) async-start(), calls=%async_computation.3 | async-start | bytes 7864320 | tf_op jit(solution)/shard_map/psum | solution.py:194
  164.0 0.7 copy-start.12
  164.0 1.4 copy-start.5
  164.0 24.9 %copy-start.14 = (s32[72]{0:T(128)S(1)}, s32[72]{0:T(128)}, u32[]{:S(2)}) copy-start(s32[72]{0:T(128)} %constant.439) | copy-start | bytes 868
  164.0 37.7 %copy-start.13 = (f32[1,128]{1,0:T(1,128)S(1)}, f32[1,128]{1,0:T(1,128)}, u32[]{:S(2)}) copy-start(f32[1,128]{1,0:T(1,128)} %param.20) | copy-start | bytes 1540
  169.0 19.9 %collective-permute-start = (f32[128]{0:T(128)S(1)}, f32[128]{0:T(128)S(1)}, u32[]{:S(2)}, u32[]{:S(2)}) collective-permute-start(f32[128]{0:T(128)S(1)} %get-tuple-element.57), channel_id=1, source_target_pairs={{0,1},{1,2},{2,3},{3,4},{4,5},{5,6},{6,7},{7,8},{8,9},{9,10},{10,1... | collective-permute-start | bytes 1544 | tf_op jit(solution)/shard_map/ppermute | solution.py:18
  171.3 21.9 %collective-permute-start.1 = (f32[128]{0:T(128)S(1)}, f32[128]{0:T(128)S(1)}, u32[]{:S(2)}, u32[]{:S(2)}) collective-permute-start(f32[128]{0:T(128)S(1)} %get-tuple-element.63), channel_id=1, source_target_pairs={{0,2},{1,3},{2,4},{3,5},{4,6},{5,7},{6,8},{7,9},{8,10},{9,11},{10,... | collective-permute-start | bytes 1544 | tf_op jit(solution)/shard_map/ppermute | solution.py:18
  175.0 22.2 %collective-permute-start.2 = (f32[128]{0:T(128)S(1)}, f32[128]{0:T(128)S(1)}, u32[]{:S(2)}, u32[]{:S(2)}) collective-permute-start(f32[128]{0:T(128)S(1)} %get-tuple-element.62), channel_id=1, source_target_pairs={{0,3},{1,4},{2,5},{3,6},{4,7},{5,8},{6,9},{7,10},{8,11},{9,12},{10... | collective-permute-start | bytes 1544 | tf_op jit(solution)/shard_map/ppermute | solution.py:18
  181.9 15.3 %collective-permute-start.3 = (f32[128]{0:T(128)S(1)}, f32[128]{0:T(128)S(1)}, u32[]{:S(2)}, u32[]{:S(2)}) collective-permute-start(f32[128]{0:T(128)S(1)} %get-tuple-element.61), channel_id=1, source_target_pairs={{0,4},{1,5},{2,6},{3,7},{4,8},{5,9},{6,10},{7,11},{8,12},{9,13},{1... | collective-permute-start | bytes 1544 | tf_op jit(solution)/shard_map/ppermute | solution.py:18
  184.1 13.2 %collective-permute-start.4 = (f32[128]{0:T(128)S(1)}, f32[128]{0:T(128)S(1)}, u32[]{:S(2)}, u32[]{:S(2)}) collective-permute-start(f32[128]{0:T(128)S(1)} %get-tuple-element.60), channel_id=1, source_target_pairs={{0,5},{1,6},{2,7},{3,8},{4,9},{5,10},{6,11},{7,12},{8,13},{9,14},{... | collective-permute-start | bytes 1544 | tf_op jit(solution)/shard_map/ppermute | solution.py:18
  188.9 10.0 %collective-permute-start.5 = (f32[128]{0:T(128)S(1)}, f32[128]{0:T(128)S(1)}, u32[]{:S(2)}, u32[]{:S(2)}) collective-permute-start(f32[128]{0:T(128)S(1)} %get-tuple-element.59), channel_id=1, source_target_pairs={{0,6},{1,7},{2,8},{3,9},{4,10},{5,11},{6,12},{7,13},{8,14},{9,15},... | collective-permute-start | bytes 1544 | tf_op jit(solution)/shard_map/ppermute | solution.py:18
  193.2 8.5 %collective-permute-start.6 = (f32[128]{0:T(128)S(1)}, f32[128]{0:T(128)S(1)}, u32[]{:S(2)}, u32[]{:S(2)}) collective-permute-start(f32[128]{0:T(128)S(1)} %get-tuple-element.58), channel_id=1, source_target_pairs={{0,7},{1,8},{2,9},{3,10},{4,11},{5,12},{6,13},{7,14},{8,15},{9,16}... | collective-permute-start | bytes 1544 | tf_op jit(solution)/shard_map/ppermute | solution.py:18
  460.3 1.0 copy-start.8
  473.2 16.6 %copy-start.9 = (f32[512,512]{1,0:T(8,128)S(1)}, f32[512,512]{1,0:T(8,128)}, u32[]{:S(2)}) copy-start(f32[512,512]{1,0:T(8,128)} %copy-done.8) | copy-start | bytes 3145732
  560.1 49.4 %copy-start.7 = (f32[512,512]{1,0:T(8,128)}, f32[512,512]{1,0:T(8,128)S(1)}, u32[]{:S(2)}) copy-start(f32[512,512]{1,0:T(8,128)S(1)} %get-tuple-element.127) | copy-start | bytes 3145732
  623.1 7.7 %copy-start.3 = (f32[2304,512]{1,0:T(8,128)S(1)}, f32[2304,512]{1,0:T(8,128)}, u32[]{:S(2)}) copy-start(f32[2304,512]{1,0:T(8,128)} %copy.63) | copy-start | bytes 14155780
  646.0 8.6 %copy-start.1 = (f32[512,128]{1,0:T(8,128)S(1)}, f32[512,128]{1,0:T(8,128)}, u32[]{:S(2)}) copy-start(f32[512,128]{1,0:T(8,128)} %param.21) | copy-start | bytes 786436
Sparse Core Ops, SparseCore 0:
  164.1 281.9 all-reduce.3
where the time goes:
time: 672 us; the launch traced here: 662 us
  waiting for transfers between devices  234 us (35%)
  other arithmetic  129 us (19%)
  blocking collectives  96.6 us (14%)
  local copies, waits for them, and re-layouts  67.5 us (10%)
  starting transfers between devices  60.7 us (9%)
  matrix products  55.5 us (8%)
  between operations  18.4 us (3%)
    psum x1, waiting for transfers between devices, per_device(): front_rows, window_rhs = lax.psum((front_rows, window_rhs), ('pts', 'grp'))  148 us
    psum x1, blocking collectives, per_device(): front_rows, window_rhs = lax.psum((front_rows, window_rhs), ('pts', 'grp'))  96.6 us
    another operation x15, other arithmetic, per_device(): factor = jnp.linalg.cholesky(square)  79.2 us
    all_to_all x1, waiting for transfers between devices, per_device(): lax.all_to_all(outgoing, 'pts', split_axis=0, concat_axis=0, tiled=True)  50.2 us
    another operation x4, other arithmetic, per_device(): panel = jax.scipy.linalg.solve_triangular(factor, columns.T, lower=True).T  43.9 us
    ppermute x7, starting transfers between devices, shifted(): return lax.ppermute(value, axis, pairs)  28 us
    all_to_all x1, waiting for transfers between devices, per_device(): lax.all_to_all(band_tiles, 'grp', split_axis=1, concat_axis=0, tiled=True)  25.5 us
    all_to_all x1, starting transfers between devices, per_device(): lax.all_to_all(outgoing, 'pts', split_axis=0, concat_axis=0, tiled=True)  24.2 us
  transfers between devices with their start and end apart: 11, of which 6 were waited for; matrix products, arithmetic and copies ran while one was open for 1% of the time, Pallas kernels for 0%

commit v1 on v0

v1 whole, which is shorter than its diff:
```python
import jax
import jax.numpy as jnp
from jax import lax
from jax.experimental import pallas as pl
from jax.experimental.pallas import tpu as pltpu
from jax.sharding import PartitionSpec as P

TOUCH = 6
BAND = 8
FRONT = 4
CR = 128
PTS = 256
COLS = 3 * PTS
NC = 512
WIN = 18
BLOCK = 16
N_BLOCKS = 32
ROWS = 8
BAND_TILES = 36
ITEMS = 56
MESH = pl.DeviceIdType.MESH
PRECISE = lax.Precision.HIGHEST
F32 = jnp.float32
BF16 = jnp.bfloat16


def band_index(row, offset):
    return row * BAND - row * (row - 1) // 2 + offset


def front_items():
    first = BAND - 1
    last = first + FRONT
    inside = [(i, j) for i in range(first, last) for j in range(i, last)]
    before = [(i, j) for i in range(first) for j in range(first, last) if j - i < BAND]
    after = [(i, j) for i in range(first, last) for j in range(last, WIN) if j - i < BAND]
    return inside + before + after


FRONT_ITEMS = front_items()
ITEM_OF = {pair: n for n, pair in enumerate(FRONT_ITEMS)}
RHS_ITEM = len(FRONT_ITEMS)
ZERO_TILE = 184
ZERO_ROW = 23


def dot_nt(a, b, precision=None):
    return lax.dot_general(a, b, (((1,), (1,)), ((), ())), precision=precision, preferred_element_type=F32)


def dot_nn(a, b, precision=None):
    return lax.dot_general(a, b, (((1,), (0,)), ((), ())), precision=precision, preferred_element_type=F32)


def dot_tn(a, b, precision=None):
    return lax.dot_general(a, b, (((0,), (0,)), ((), ())), precision=precision, preferred_element_type=F32)


def invert_blocks(blocks):
    diag_x, diag_y, diag_z = blocks[0:1], blocks[1:2], blocks[2:3]
    cross_xy, cross_xz, cross_yz = blocks[3:4], blocks[4:5], blocks[5:6]
    adj_xx = diag_y * diag_z - cross_yz * cross_yz
    adj_yy = diag_x * diag_z - cross_xz * cross_xz
    adj_zz = diag_x * diag_y - cross_xy * cross_xy
    adj_xy = cross_xz * cross_yz - cross_xy * diag_z
    adj_xz = cross_xy * cross_yz - diag_y * cross_xz
    adj_yz = cross_xy * cross_xz - diag_x * cross_yz
    determinant = diag_x * adj_xx + cross_xy * adj_xy + cross_xz * adj_xz
    inverse_det = 1.0 / determinant
    return [
        [adj_xx * inverse_det, adj_xy * inverse_det, adj_xz * inverse_det],
        [adj_xy * inverse_det, adj_yy * inverse_det, adj_yz * inverse_det],
        [adj_xz * inverse_det, adj_yz * inverse_det, adj_zz * inverse_det],
    ]


def pair_kernel(inc, owner, first, jac, blocks, grad, cam, damp, band, table, jac_band, scl_band):
    device = lax.axis_index("pts") * 4 + lax.axis_index("grp")
    my_block = device // BLOCK

    @pl.loop(0, 128)
    def _(r):
        table[owner[r]] = r

    start = first[0] + NC - (BAND - 1)
    for n, (row, col) in enumerate(FRONT_ITEMS):
        cluster = (start + row) % NC
        spot = (cluster % BLOCK) * BAND + (col - row)
        table[128 + n] = jnp.where(cluster // BLOCK == my_block, spot, ZERO_TILE)
    for n in range(RHS_ITEM, 64):
        table[128 + n] = ZERO_TILE
    for j in range(FRONT):
        cluster = (first[0] + j) % NC
        table[192 + j] = jnp.where(cluster // BLOCK == my_block, cluster % BLOCK, ZERO_ROW)

    inverse = invert_blocks(blocks[...])
    zero = jnp.zeros((CR, COLS), BF16)
    for a in range(BAND):
        jac_band[a] = zero
        scl_band[a] = zero
    for k in range(TOUCH):
        slot = (inc[k] + NC - device) % NC
        jac_band[slot] = jac[k]
        wide = [jac[k, :, PTS * c : PTS * (c + 1)].astype(F32) for c in range(3)]
        for c in range(3):
            summed = wide[0] * inverse[0][c]
            summed = summed + wide[1] * inverse[1][c]
            summed = summed + wide[2] * inverse[2][c]
            scl_band[slot, :, PTS * c : PTS * (c + 1)] = summed.astype(BF16)

    for a in range(BAND):
        for b in range(a, BAND):
            tile = dot_nt(scl_band[a], jac_band[b])
            if a == 0 and b == 0:
                row = lax.broadcasted_iota(jnp.int32, (CR, CR), 0)
                col = lax.broadcasted_iota(jnp.int32, (CR, CR), 1)
                tile = tile + jnp.where(row == col, damp[...], 0.0)
            band[band_index(a, b - a)] = tile
    grad8 = jnp.broadcast_to(grad[...], (16, COLS))
    rows = []
    for a in range(BAND):
        pulled = dot_nt(grad8, scl_band[a])[0:1]
        rows.append(cam[...] - pulled if a == 0 else -pulled)
    chunk = jnp.concatenate(rows, axis=0)
    for j in range(16):
        band[BAND_TILES, ROWS * j : ROWS * (j + 1)] = chunk


def exchange_kernel(
    table, band, owned, wide, mine, parts, tiles, carried, sums, sums_in, sorted_tiles, fronts, spread, gathered, sem, all_sem
):
    pts = lax.axis_index("pts")
    grp = lax.axis_index("grp")
    block = pts // 4
    low = pts % 4
    core = low % 2
    depth = low // 2
    me = 4 * low + grp
    my_rows = core * 8 + depth * 4 + grp
    row0 = pl.multiple_of(ROWS * my_rows, ROWS)

    @pl.loop(0, BLOCK)
    def _(step):
        peer = (me + step) % BLOCK
        p_low = peer // 4
        p_grp = peer % 4
        rows = (p_low % 2) * 8 + (p_low // 2) * 4 + p_grp
        src = band.at[:, pl.ds(pl.multiple_of(ROWS * rows, ROWS), ROWS), :]

        @pl.when(step == 0)
        def _():
            pltpu.make_async_copy(src, parts.at[7 + me], sem.at[1]).start()

        @pl.when(step > 0)
        def _():
            pltpu.make_async_remote_copy(
                src_ref=src,
                dst_ref=parts.at[7 + me],
                send_sem=sem.at[0],
                recv_sem=sem.at[1],
                device_id=(block * 4 + p_low, p_grp),
                device_id_type=MESH,
            ).start()

    blank = jnp.zeros((ROWS, CR), F32)

    @pl.loop(0, BAND_TILES + 1)
    def _(n):
        for q in range(7):
            parts[q, n] = blank
            parts[23 + q, n] = blank

    tiles[ZERO_TILE] = blank
    pltpu.make_async_copy(parts.at[pl.ds(7, BLOCK)], parts.at[pl.ds(7, BLOCK)], sem.at[1]).wait()

    def add_up(b):
        for d in range(BAND):
            total = parts[b + 7, band_index(0, d)]
            for a in range(1, BAND - d):
                total = total + parts[b - a + 7, band_index(a, d)]
            tiles[b * BAND + d] = total
        line = parts[b + 7, BAND_TILES, 0:1]
        for a in range(1, BAND):
            line = line + parts[b - a + 7, BAND_TILES, a : a + 1]
        sums[pl.ds(b, 1)] = line

    sums[pl.ds(16, 8)] = blank
    pl.loop(BLOCK, BLOCK + 7)(add_up)
    ahead = (block + 1) % N_BLOCKS
    carry = pltpu.make_async_remote_copy(
        src_ref=tiles.at[pl.ds(128, 56)],
        dst_ref=carried,
        send_sem=sem.at[2],
        recv_sem=sem.at[3],
        device_id=(ahead * 4 + low, grp),
        device_id_type=MESH,
    )
    carry.start()
    carry_sums = pltpu.make_async_remote_copy(
        src_ref=sums.at[pl.ds(16, 8)],
        dst_ref=sums_in,
        send_sem=sem.at[4],
        recv_sem=sem.at[5],
        device_id=(ahead * 4 + low, grp),
        device_id_type=MESH,
    )
    carry_sums.start()
    pl.loop(0, BLOCK)(add_up)
    carry.wait()
    carry_sums.wait()
    for b in range(7):
        for d in range(7 - b):
            tiles[b * BAND + d] = tiles[b * BAND + d] + carried[b * BAND + d]
    sums[0:8] = sums[0:8] + sums_in[...]
    mine[...] = jnp.broadcast_to(sums[pl.ds(me, 1)], (ROWS, CR))

    @pl.loop(0, 64)
    def _(n):
        fronts[n] = tiles[table[128 + n]]

    for j in range(FRONT):
        fronts[RHS_ITEM, j : j + 1] = sums[pl.ds(table[192 + j], 1)]

    @pl.loop(1, N_BLOCKS)
    def _(step):
        other = (block + step) % N_BLOCKS
        pltpu.make_async_remote_copy(
            src_ref=fronts.at[pl.ds(2 * other, 2)],
            dst_ref=spread.at[block],
            send_sem=sem.at[6],
            recv_sem=sem.at[7],
            device_id=(other * 4 + low, grp),
            device_id_type=MESH,
        ).start()

    spread[block] = fronts[pl.ds(2 * block, 2)]

    @pl.loop(0, 128)
    def _(o):
        sorted_tiles[o] = tiles[table[o]]

    to_grp = block // 8
    slot = block % 8

    @pl.loop(0, 128)
    def _(step):
        o = (pts + step) % 128
        here = jnp.logical_and(step == 0, to_grp == grp)
        dst = owned.at[slot, pl.ds(row0, ROWS), :]

        @pl.when(here)
        def _():
            pltpu.make_async_copy(sorted_tiles.at[o], dst, all_sem.at[1]).start()

        @pl.when(jnp.logical_not(here))
        def _():
            pltpu.make_async_remote_copy(
                src_ref=sorted_tiles.at[o],
                dst_ref=dst,
                send_sem=all_sem.at[0],
                recv_sem=all_sem.at[1],
                device_id=(o, to_grp),
                device_id_type=MESH,
            ).start()

    def await_bytes(ref, which):
        pltpu.make_async_copy(ref, ref, which).wait()

    await_bytes(spread.at[pl.ds(0, N_BLOCKS - 1)], sem.at[7])
    for i in range(2):
        total = spread[0, i]
        for b in range(1, N_BLOCKS):
            total = total + spread[b, i]
        gathered[2 * block + i] = total

    @pl.loop(1, N_BLOCKS)
    def _(step):
        other = (block + step) % N_BLOCKS
        pltpu.make_async_remote_copy(
            src_ref=gathered.at[pl.ds(2 * block, 2)],
            dst_ref=gathered.at[pl.ds(2 * block, 2)],
            send_sem=sem.at[8],
            recv_sem=sem.at[9],
            device_id=(other * 4 + low, grp),
            device_id_type=MESH,
        ).start()

    await_bytes(spread.at[pl.ds(0, N_BLOCKS - 1)], sem.at[9])

    rows8 = wide.at[:, pl.ds(row0, ROWS), :]
    for step in range(4):
        if step == 0:
            pltpu.make_async_copy(gathered.at[pl.ds(0, ITEMS)], rows8, sem.at[11]).start()
        else:
            pltpu.make_async_remote_copy(
                src_ref=gathered.at[pl.ds(0, ITEMS)],
                dst_ref=rows8,
                send_sem=sem.at[10],
                recv_sem=sem.at[11],
                device_id=(pts, (grp + step) % 4),
                device_id_type=MESH,
            ).start()
    row32 = pl.multiple_of(core * 64 + depth * 32, 32)
    await_bytes(wide.at[:, pl.ds(row32, 32), :], sem.at[11])
    along_z = pltpu.make_async_remote_copy(
        src_ref=wide.at[:, pl.ds(row32, 32), :],
        dst_ref=wide.at[:, pl.ds(row32, 32), :],
        send_sem=sem.at[12],
        recv_sem=sem.at[13],
        device_id=(pts + 2 - 4 * depth, grp),
        device_id_type=MESH,
    )
    along_z.start()
    along_z.wait()
    row64 = pl.multiple_of(core * 64, 64)
    to_core = pltpu.make_async_remote_copy(
        src_ref=wide.at[:, pl.ds(row64, 64), :],
        dst_ref=wide.at[:, pl.ds(row64, 64), :],
        send_sem=sem.at[14],
        recv_sem=sem.at[15],
        device_id=(pts + 1 - 2 * core, grp),
        device_id_type=MESH,
    )
    to_core.start()
    to_core.wait()

    await_bytes(parts.at[pl.ds(0, BLOCK - 1)], sem.at[0])
    await_bytes(spread.at[pl.ds(0, N_BLOCKS - 1)], sem.at[6])
    await_bytes(spread.at[pl.ds(0, N_BLOCKS - 1)], sem.at[8])
    await_bytes(wide.at[:, pl.ds(0, 24), :], sem.at[10])

    @pl.when(to_grp == grp)
    def _():
        await_bytes(sorted_tiles.at[pl.ds(0, 127)], all_sem.at[0])

    @pl.when(to_grp != grp)
    def _():
        await_bytes(sorted_tiles, all_sem.at[0])

    await_bytes(owned, all_sem.at[1])


def factor_rows(block, out_upper, out_inverse):
    count = CR // ROWS
    sub = lax.broadcasted_iota(jnp.int32, (ROWS, CR), 0)
    lane = lax.broadcasted_iota(jnp.int32, (ROWS, CR), 1)
    left = [block[ROWS * s : ROWS * (s + 1)] for s in range(count)]
    right = [jnp.where(sub + ROWS * s == lane, 1.0, 0.0).astype(F32) for s in range(count)]

    def across(value, column):
        return jnp.broadcast_to(value[:, column : column + 1], (ROWS, CR))

    def down(value, row):
        return jnp.broadcast_to(value[row : row + 1], (ROWS, CR))

    for b in range(count):
        base = ROWS * b
        cols = [across(left[b], base + k) for k in range(ROWS)]
        e = [[down(cols[j], i) if j <= i else None for j in range(ROWS)] for i in range(ROWS)]
        x = [down(left[b], i) for i in range(ROWS)]
        y = [down(right[b], i) for i in range(ROWS)]
        inv = []
        for j in range(ROWS):
            scale = lax.rsqrt(e[j][j])
            inv.append(scale)
            for i in range(j + 1, ROWS):
                e[i][j] = e[i][j] * scale
            x[j] = x[j] * scale
            y[j] = y[j] * scale
            for i in range(j + 1, ROWS):
                for k in range(j + 1, i + 1):
                    e[i][k] = e[i][k] - e[i][j] * e[k][j]
                x[i] = x[i] - e[i][j] * x[j]
                y[i] = y[i] - e[i][j] * y[j]
        for j in range(ROWS):
            out_upper[base + j : base + j + 1] = x[j][0:1]
            out_inverse[base + j : base + j + 1] = y[j][0:1]
        if b == count - 1:
            break
        xs = [None] * ROWS
        ys = [None] * ROWS
        for j in reversed(range(ROWS)):
            px, py = x[j], y[j]
            for i in range(j + 1, ROWS):
                px = px - e[i][j] * xs[i]
                py = py - e[i][j] * ys[i]
            xs[j] = px * inv[j]
            ys[j] = py * inv[j]
        for s in range(b + 1, count):
            ratios = [across(left[s], base + k) for k in range(ROWS)]
            for k in range(ROWS):
                left[s] = left[s] - ratios[k] * xs[k]
                right[s] = right[s] - ratios[k] * ys[k]


def front_kernel(
    table, first, owned_hbm, wide, mine, tiles_hbm, rhs, panel, square, upper, inverse, rows_of, owned, sem
):
    pts = lax.axis_index("pts")
    grp = lax.axis_index("grp")
    fetch = pltpu.make_async_copy(owned_hbm, owned, sem.at[0])
    fetch.start()
    nil = jnp.zeros((CR, CR), F32)
    lead = BAND - 1
    for i in range(FRONT):
        for j in range(i, FRONT):
            square[i, j] = wide[ITEM_OF[lead + i, lead + j]]
        inverse[i] = jnp.zeros((CR, FRONT * CR), F32)

    for i in range(WIN):
        for j in range(FRONT):
            f = lead + j
            if i < lead:
                piece = wide[ITEM_OF[i, f]] if (i, f) in ITEM_OF else nil
            elif i >= lead + FRONT:
                piece = wide[ITEM_OF[f, i]].T if (f, i) in ITEM_OF else nil
            else:
                continue
            rows_of[i, :, CR * j : CR * (j + 1)] = piece

    row = lax.broadcasted_iota(jnp.int32, (CR, CR), 0)
    col = lax.broadcasted_iota(jnp.int32, (CR, CR), 1)

    @pl.loop(0, FRONT)
    def _(k):
        at = pl.multiple_of(CR * k, CR)
        factor_rows(square[k, k], upper.at[k], upper.at[FRONT])
        own = upper[FRONT]
        upper[k] = jnp.where(row <= col, upper[k], 0.0)
        so_far = inverse[k]
        done = dot_nn(own, so_far, PRECISE)
        inverse[k] = done
        inverse[k, :, pl.ds(at, CR)] = own
        for j in range(1, FRONT):

            @pl.when(j > k)
            def _():
                square[k, j] = dot_nn(own, square[k, j], PRECISE)

        for i in range(1, FRONT):

            @pl.when(i > k)
            def _():
                lower = square[k, i]
                inverse[i] = inverse[i] - dot_tn(lower, inverse[k], PRECISE)
                for j in range(i, FRONT):
                    square[i, j] = square[i, j] - dot_tn(lower, square[k, j], PRECISE)

    part = inverse[grp]
    for i in range(WIN):
        if lead <= i < lead + FRONT:
            j = i - lead

            @pl.when(grp == j)
            def _():
                panel[CR * i : CR * (i + 1)] = upper[j].T

            @pl.when(grp < j)
            def _():
                panel[CR * i : CR * (i + 1)] = square[grp, j].T

            @pl.when(grp > j)
            def _():
                panel[CR * i : CR * (i + 1)] = nil
        else:
            panel[CR * i : CR * (i + 1)] = dot_nt(rows_of[i], part, PRECISE)

    base = first[0] + NC - lead
    device = pts * 4 + grp
    stacked = jnp.concatenate([wide[RHS_ITEM, j : j + 1] for j in range(FRONT)], axis=1)
    stacked = jnp.broadcast_to(stacked, (ROWS, FRONT * CR))
    solved = [dot_nt(stacked, inverse[j], PRECISE) for j in range(FRONT)]
    spot = (device + NC - base % NC) % NC
    rhs[...] = mine[0:1]
    for j in range(FRONT):

        @pl.when(spot == lead + j)
        def _():
            rhs[...] = solved[j][0:1]

    in_rest = jnp.logical_and(spot < WIN, jnp.logical_or(spot < lead, spot >= lead + FRONT))

    @pl.when(in_rest)
    def _():
        at = jnp.minimum(spot, WIN - 1)
        total = dot_nn(solved[0], inverse[0], PRECISE)
        for j in range(1, FRONT):
            total = total + dot_nn(solved[j], inverse[j], PRECISE)
        rhs[...] = mine[0:1] - dot_nt(total, rows_of[at], PRECISE)[0:1]

    fetch.wait()
    residue = table[pts]
    ahead = residue % BAND
    near = (residue // BAND + BLOCK - base % BLOCK) % BLOCK
    for extra in range(2):
        one = near + BLOCK * extra
        two = one + ahead
        cluster = (base + one) % NC
        fits = jnp.logical_and(two < WIN, cluster // 128 == grp)
        for p in (one, two):
            fits = jnp.logical_and(fits, jnp.logical_or(p < lead, p >= lead + FRONT))

        @pl.when(fits)
        def _():
            slot = (cluster // BLOCK) % 8
            a = rows_of[jnp.minimum(one, WIN - 1)]
            b = rows_of[jnp.minimum(two, WIN - 1)]
            change = nil
            for j in range(FRONT):
                change = change + dot_nt(dot_nt(a, inverse[j], PRECISE), dot_nt(b, inverse[j], PRECISE), PRECISE)
            owned[slot] = owned[slot] - change

    store = pltpu.make_async_copy(owned, tiles_hbm, sem.at[1])
    store.start()
    store.wait()


def vmem_spec():
    return pl.BlockSpec(memory_space=pltpu.VMEM)


def smem_spec():
    return pl.BlockSpec(memory_space=pltpu.SMEM)


def any_spec():
    return pl.BlockSpec(memory_space=pl.ANY)


def shape(*dims, dtype=F32):
    return jax.ShapeDtypeStruct(dims, dtype)


def per_device(jacobian, point_blocks, point_grad, camera_grad, damping, incidence, tile_owner, front_first):
    device = lax.axis_index("pts") * 4 + lax.axis_index("grp")
    jac = jacobian.reshape(TOUCH, CR, COLS)
    damp = lax.dynamic_slice_in_dim(damping, device, 1, 0)
    band, table = pl.pallas_call(
        pair_kernel,
        out_shape=(shape(BAND_TILES + 1, CR, CR), shape(256, dtype=jnp.int32)),
        in_specs=[smem_spec()] * 3 + [vmem_spec()] * 5,
        out_specs=(vmem_spec(), smem_spec()),
        scratch_shapes=[pltpu.VMEM((BAND, CR, COLS), BF16), pltpu.VMEM((BAND, CR, COLS), BF16)],
        compiler_params=pltpu.CompilerParams(vmem_limit_bytes=40 * 2**20),
        name="pairs",
    )(
        incidence.reshape(TOUCH),
        tile_owner,
        front_first,
        jac,
        point_blocks.reshape(6, PTS),
        point_grad.reshape(1, COLS),
        camera_grad,
        damp,
    )
    owned, wide, mine = pl.pallas_call(
        exchange_kernel,
        out_shape=(shape(8, CR, CR), shape(ITEMS, CR, CR), shape(ROWS, CR)),
        in_specs=[smem_spec(), any_spec()],
        out_specs=(any_spec(), any_spec(), vmem_spec()),
        scratch_shapes=[
            pltpu.VMEM((30, BAND_TILES + 1, ROWS, CR), F32),
            pltpu.VMEM((185, ROWS, CR), F32),
            pltpu.VMEM((56, ROWS, CR), F32),
            pltpu.VMEM((24, CR), F32),
            pltpu.VMEM((ROWS, CR), F32),
            pltpu.VMEM((128, ROWS, CR), F32),
            pltpu.VMEM((64, ROWS, CR), F32),
            pltpu.VMEM((N_BLOCKS, 2, ROWS, CR), F32),
            pltpu.VMEM((64, ROWS, CR), F32),
            pltpu.SemaphoreType.DMA((16,)),
            pltpu.SemaphoreType.DMA((2,)),
        ],
        compiler_params=pltpu.CompilerParams(vmem_limit_bytes=40 * 2**20, has_side_effects=True),
        name="exchange",
    )(table, band)
    return pl.pallas_call(
        front_kernel,
        out_shape=(shape(8, CR, CR), shape(1, CR), shape(WIN * CR, CR)),
        in_specs=[smem_spec(), smem_spec(), any_spec(), vmem_spec(), vmem_spec()],
        out_specs=(any_spec(), vmem_spec(), vmem_spec()),
        scratch_shapes=[
            pltpu.VMEM((FRONT, FRONT, CR, CR), F32),
            pltpu.VMEM((FRONT + 1, CR, CR), F32),
            pltpu.VMEM((FRONT, CR, FRONT * CR), F32),
            pltpu.VMEM((WIN, CR, FRONT * CR), F32),
            pltpu.VMEM((8, CR, CR), F32),
            pltpu.SemaphoreType.DMA((2,)),
        ],
        compiler_params=pltpu.CompilerParams(vmem_limit_bytes=40 * 2**20),
        name="front",
    )(table, front_first, owned, wide, mine)


def solution(mesh):
    in_specs = (
        P(("pts", "grp"), None, None, None, None),
        P(("pts", "grp"), None, None),
        P(("pts", "grp"), None, None),
        P(("pts", "grp"), None),
        P(),
        P(("pts", "grp"), None),
        P(),
        P(),
    )
    out_specs = (P(("pts", "grp"), None, None), P(("pts", "grp"), None), P(None, "grp"))
    return jax.shard_map(per_device, mesh=mesh, in_specs=in_specs, out_specs=out_specs, check_vma=False)
```

time: 672 us -> 189 us (0.28); the launches traced: 662 us -> 186 us
  waiting for transfers between devices: 234 us -> 0 us
  Pallas kernels: 0 us -> 181 us
  other arithmetic: 129 us -> 0 us
  blocking collectives: 96.6 us -> 0 us
  local copies, waits for them, and re-layouts: 67.5 us -> 4 us
  starting transfers between devices: 60.7 us -> 0 us
  matrix products: 55.5 us -> 0 us
  between operations: 18.4 us -> 1.55 us
    pallas_call x0 -> x3, Pallas kernels: none -> 181 us  [the longest x1 136 us: per_device(): pl.pallas_call(exchange_kernel, out_shape=(shape(8, CR, CR), shape(ITEMS,...]
    psum x1 -> x0, waiting for transfers between devices: 148 us -> none  [per_device(): front_rows, window_rhs = lax.psum((front_rows, window_rhs), ('pts', 'grp'))]
    another operation x22 -> x0, other arithmetic: 125 us -> none  [the longest x15 79.2 us: per_device(): factor = jnp.linalg.cholesky(square)]
    psum x1 -> x0, blocking collectives: 96.6 us -> none  [per_device(): front_rows, window_rhs = lax.psum((front_rows, window_rhs), ('pts', 'grp'))]
    all_to_all x3 -> x0, waiting for transfers between devices: 81.6 us -> none  [the longest x1 50.2 us: per_device(): lax.all_to_all(outgoing, 'pts', split_axis=0, concat_axis=0, tiled=True)]
    dot_general x14 -> x0, matrix products: 40.2 us -> none  [the longest x1 7.71 us: per_device(): jnp.einsum('sp,pra->sra', pick_home, panel_blocks, precision=PRECISE)]
    all_to_all x3 -> x0, starting transfers between devices: 32.7 us -> none  [the longest x1 24.2 us: per_device(): lax.all_to_all(outgoing, 'pts', split_axis=0, concat_axis=0, tiled=True)]
    ppermute x7 -> x0, starting transfers between devices: 28 us -> none  [shifted(): return lax.ppermute(value, axis, pairs)]
  transfers between devices with their start and end apart: 11 -> 0, of which waited for: 6 -> 0; matrix products, arithmetic and copies ran while one was open for 1% -> 0% of each run, Pallas kernels for 0% -> 0%
where the time goes in v1:
time: 189 us; the launch traced here: 186 us
  Pallas kernels  181 us (96%)
  local copies, waits for them, and re-layouts  4 us (2%)
    pallas_call x1, Pallas kernels, per_device(): pl.pallas_call(exchange_kernel, out_shape=(shape(8, CR, CR), shape(ITEMS,...  136 us
    pallas_call x1, Pallas kernels, per_device(): pl.pallas_call(front_kernel, out_shape=(shape(8, CR, CR), shape(1, CR), s...  39.3 us
    pallas_call x1, Pallas kernels, per_device(): pl.pallas_call(pair_kernel, out_shape=(shape(BAND_TILES + 1, CR, CR), sha...  5.65 us

profile of v1, /device:TPU:1, one launch (start us, length us, event | category | flops | bytes accessed | tf_op | source)
XLA Modules:
  0.0 186.4 jit_solution(14420280093379138416)
XLA Ops:
  0.6 0.0 copy-start
  1.3 0.3 copy-done
  1.6 0.7 copy.15
  2.3 0.7 copy.17
  3.0 1.7 copy.12
  4.7 0.0 copy-start.1
  4.7 0.0 copy-start.2
  4.7 0.0 copy-start.3
  4.7 0.6 copy.13.jac
  5.3 0.0 copy-done.1
  5.3 0.0 copy-done.2
  5.4 0.0 copy-done.3
  5.4 5.6 %pairs.1 = (f32[37,128,128]{2,1,0:T(8,128)S(1)}, s32[256]{0:T(256)S(1)}) custom-call(s32[6]{0:T(128)S(1)} %bitcast.9, s32[128]{0:T(128)S(1)} %copy-done.2, s32[1]{0:T(128)S(6)} %copy.18.first, bf16[6,128,768]{2,1,0:T(8,128)(2,1)S(1)} %copy.13.jac, f32[6,256]{1,0:T(8,128)S(1)} %bitcast.7, bf16[1,768]{1,0:T(2,128)(2,1)S(1)} %bitcast.8, ...), custom_call_target="tpu_custom_call" | custom-call | tf_op jit(solution)/shard_map/pairs/pallas_call | solution.py:538
  11.0 135.9 %exchange.1 = (f32[8,128,128]{2,1,0:T(8,128)S(1)}, f32[56,128,128]{2,1,0:T(8,128)S(1)}, f32[8,128]{1,0:T(8,128)S(1)}) custom-call(s32[256]{0:T(256)S(1)} %get-tuple-element.8.table, f32[37,128,128]{2,1,0:T(8,128)S(1)} %get-tuple-element.9.band), custom_call_target="tpu_custom_call" | custom-call | tf_op jit(solution)/shard_map/exchange/pallas_call | solution.py:556
  146.9 39.3 %front.1 = (f32[8,128,128]{2,1,0:T(8,128)}, f32[1,128]{1,0:T(1,128)}, f32[2304,128]{1,0:T(8,128)}) custom-call(s32[256]{0:T(256)S(1)} %get-tuple-element.8.table, s32[1]{0:T(128)S(6)} %copy.18.first, f32[8,128,128]{2,1,0:T(8,128)S(1)} %get-tuple-element.10.owned_hbm, f32[56,128,128]{2,1,0:T(8,128)S(1)} %get-tuple-element.11.wide, ...), custom_call_target="tpu_custom_call" | custom-call | tf_op jit(solution)/shard_map/front/pallas_call | solution.py:577
  (1 shorter events, 0.0 us)
Async XLA Ops:
  0.6 1.0 copy-start
  4.7 0.7 copy-start.1
  4.7 0.7 copy-start.2
  4.7 0.7 copy-start.3

commit v2 on v1

v2 whole, which is shorter than its diff:
```python
import jax
import jax.numpy as jnp
from jax import lax
from jax.experimental import pallas as pl
from jax.experimental.pallas import tpu as pltpu
from jax.sharding import PartitionSpec as P

TOUCH = 6
BAND = 8
FRONT = 4
CR = 128
PTS = 256
COLS = 3 * PTS
NC = 512
WIN = 18
BLOCK = 16
N_BLOCKS = 32
ROWS = 8
TILES = 21
NONE = 64
INNER = 11
OUTER = 44
MESH = pl.DeviceIdType.MESH
PRECISE = lax.Precision.HIGHEST
F32 = jnp.float32
BF16 = jnp.bfloat16


def tile_index(i, j):
    return (TOUCH - 1) * i - i * (i - 1) // 2 + j


def front_items():
    first = BAND - 1
    last = first + FRONT
    inside = [(i, j) for i in range(first, last) for j in range(i, last)]
    before = [(i, j) for i in range(first) for j in range(first, last) if j - i < BAND]
    after = [(i, j) for i in range(first, last) for j in range(last, WIN) if j - i < BAND]
    return inside + before + after


FRONT_ITEMS = front_items()
RHS_ITEM = 10
OUTER_OF = {pair: n - 10 for n, pair in enumerate(FRONT_ITEMS) if n >= 10}
INNER_OF = {pair: n for n, pair in enumerate(FRONT_ITEMS) if n < 10}
ZERO_TILE = 184
ZERO_ROW = 23


def dot_nt(a, b, precision=None):
    return lax.dot_general(a, b, (((1,), (1,)), ((), ())), precision=precision, preferred_element_type=F32)


def dot_nn(a, b, precision=None):
    return lax.dot_general(a, b, (((1,), (0,)), ((), ())), precision=precision, preferred_element_type=F32)


def dot_tn(a, b, precision=None):
    return lax.dot_general(a, b, (((0,), (0,)), ((), ())), precision=precision, preferred_element_type=F32)


def invert_blocks(blocks):
    diag_x, diag_y, diag_z = blocks[0:1], blocks[1:2], blocks[2:3]
    cross_xy, cross_xz, cross_yz = blocks[3:4], blocks[4:5], blocks[5:6]
    adj_xx = diag_y * diag_z - cross_yz * cross_yz
    adj_yy = diag_x * diag_z - cross_xz * cross_xz
    adj_zz = diag_x * diag_y - cross_xy * cross_xy
    adj_xy = cross_xz * cross_yz - cross_xy * diag_z
    adj_xz = cross_xy * cross_yz - diag_y * cross_xz
    adj_yz = cross_xy * cross_xz - diag_x * cross_yz
    determinant = diag_x * adj_xx + cross_xy * adj_xy + cross_xz * adj_xz
    inverse_det = 1.0 / determinant
    return [
        [adj_xx * inverse_det, adj_xy * inverse_det, adj_xz * inverse_det],
        [adj_xy * inverse_det, adj_yy * inverse_det, adj_yz * inverse_det],
        [adj_xz * inverse_det, adj_yz * inverse_det, adj_zz * inverse_det],
    ]


def pair_kernel(inc, owner, first, jac, blocks, grad, cam, band, places, table, jac_sorted, scl_sorted):
    device = lax.axis_index("pts") * 4 + lax.axis_index("grp")
    my_block = device // BLOCK

    @pl.loop(0, 128)
    def _(r):
        table[owner[r]] = r

    start = first[0] + NC - (BAND - 1)
    for n, (row, col) in enumerate(FRONT_ITEMS):
        cluster = (start + row) % NC
        spot = (cluster % BLOCK) * BAND + (col - row)
        table[128 + n + (n >= RHS_ITEM)] = jnp.where(cluster // BLOCK == my_block, spot, ZERO_TILE)
    for n in (RHS_ITEM, *range(len(FRONT_ITEMS) + 1, 64)):
        table[128 + n] = ZERO_TILE
    for j in range(FRONT):
        cluster = (first[0] + j) % NC
        table[192 + j] = jnp.where(cluster // BLOCK == my_block, cluster % BLOCK, ZERO_ROW)

    inverse = invert_blocks(blocks[...])
    slots = [(inc[k] + NC - device) % NC for k in range(TOUCH)]
    lane = lax.broadcasted_iota(jnp.int32, (ROWS, CR), 1)
    place = jnp.full((ROWS, CR), NONE, jnp.int32)
    for k in range(TOUCH):
        rank = jnp.int32(0)
        for other in range(TOUCH):
            if other != k:
                rank = rank + (slots[other] < slots[k]).astype(jnp.int32)
        place = jnp.where(lane == slots[k], tile_index(rank, 0), place)
        place = jnp.where(lane == slots[k] + BAND, rank, place)
        jac_sorted[rank] = jac[k]
        wide = [jac[k, :, PTS * c : PTS * (c + 1)].astype(F32) for c in range(3)]
        for c in range(3):
            summed = wide[0] * inverse[0][c]
            summed = summed + wide[1] * inverse[1][c]
            summed = summed + wide[2] * inverse[2][c]
            scl_sorted[rank, :, PTS * c : PTS * (c + 1)] = summed.astype(BF16)
    places[...] = place

    for i in range(TOUCH):
        for j in range(i, TOUCH):
            band[tile_index(i, j)] = dot_nt(scl_sorted[i], jac_sorted[j])
    grad16 = jnp.broadcast_to(grad[...], (16, COLS))
    rows = [-dot_nt(grad16, scl_sorted[i])[0:1] for i in range(TOUCH)]
    chunk = jnp.concatenate([*rows, cam[...], jnp.zeros((1, CR), F32)], axis=0)
    for j in range(16):
        band[TILES, ROWS * j : ROWS * (j + 1)] = chunk


def exchange_kernel(
    table,
    band,
    places,
    damp,
    owned,
    outer,
    mine,
    stacked,
    inverse,
    across_me,
    parts,
    places_in,
    tiles,
    carried,
    sums,
    sums_in,
    sorted_tiles,
    fronts,
    spread,
    gathered,
    inner,
    square,
    upper,
    spots,
    sem,
    all_sem,
):
    pts = lax.axis_index("pts")
    grp = lax.axis_index("grp")
    block = pts // 4
    low = pts % 4
    core = low % 2
    depth = low // 2
    me = 4 * low + grp
    my_rows = core * 8 + depth * 4 + grp
    row0 = pl.multiple_of(ROWS * my_rows, ROWS)
    row32 = pl.multiple_of(core * 64 + depth * 32, 32)
    row64 = pl.multiple_of(core * 64, 64)
    z = (pts // 2) % 8
    above = pts - 2 * z + 2 * ((z + 1) % 8)
    below = pts - 2 * z + 2 * ((z + 7) % 8)
    other_core = pts + 1 - 2 * core

    def send(src, dst, out, arrive, to_pts, to_grp):
        copy = pltpu.make_async_remote_copy(
            src_ref=src, dst_ref=dst, send_sem=out, recv_sem=arrive, device_id=(to_pts, to_grp), device_id_type=MESH
        )
        copy.start()
        return copy

    def await_bytes(ref, which):
        pltpu.make_async_copy(ref, ref, which).wait()

    barrier = pltpu.get_barrier_semaphore()

    @pl.loop(1, BLOCK)
    def _(step):
        peer = (me + step) % BLOCK
        pl.semaphore_signal(barrier, inc=1, device_id=(block * 4 + peer // 4, peer % 4), device_id_type=MESH)

    @pl.loop(1, N_BLOCKS)
    def _(step):
        other = (block + step) % N_BLOCKS
        pl.semaphore_signal(barrier, inc=1, device_id=(other * 4 + low, grp), device_id_type=MESH)

    blank = jnp.zeros((ROWS, CR), F32)

    @pl.loop(0, 30)
    def _(q):
        parts[q, TILES + 1] = blank

    for q in (*range(7), *range(23, 30)):
        parts[q, TILES] = blank

        @pl.loop(0, 2 * BAND)
        def _(n):
            spots[q, n] = NONE

    tiles[ZERO_TILE] = blank
    pl.semaphore_wait(barrier, BLOCK - 1 + N_BLOCKS - 1)

    pltpu.make_async_copy(places, places_in.at[me], sem.at[23]).start()
    pltpu.make_async_copy(band.at[:, pl.ds(row0, ROWS), :], parts.at[7 + me, pl.ds(0, TILES + 1)], sem.at[1]).start()

    @pl.loop(1, BLOCK)
    def _(step):
        peer = (me + step) % BLOCK
        p_low = peer // 4
        p_grp = peer % 4
        rows = (p_low % 2) * 8 + (p_low // 2) * 4 + p_grp
        send(places, places_in.at[me], sem.at[22], sem.at[23], block * 4 + p_low, p_grp)
        src = band.at[:, pl.ds(pl.multiple_of(ROWS * rows, ROWS), ROWS), :]
        send(src, parts.at[7 + me, pl.ds(0, TILES + 1)], sem.at[0], sem.at[1], block * 4 + p_low, p_grp)

    await_bytes(places_in, sem.at[23])
    to_scalars = pltpu.make_async_copy(places_in.at[:, 0, :], spots.at[pl.ds(7, BLOCK)], sem.at[24])
    to_scalars.start()
    to_scalars.wait()
    await_bytes(parts.at[pl.ds(7, BLOCK), pl.ds(0, TILES + 1)], sem.at[1])

    sub = lax.broadcasted_iota(jnp.int32, (ROWS, CR), 0)
    lane = lax.broadcasted_iota(jnp.int32, (ROWS, CR), 1)

    def add_up(b, own):
        totals = [None] * BAND
        line = None
        for a in range(BAND):
            q = b - a + 7
            here = spots[q, a]
            for d in range(BAND - a):
                value = parts[q, jnp.minimum(here + spots[q, BAND + a + d], TILES + 1)]
                totals[d] = value if totals[d] is None else totals[d] + value
            row = parts[q, TILES, pl.ds(jnp.minimum(spots[q, BAND + a], 7), 1)]
            line = row if line is None else line + row
        if own:
            line = line + parts[b + 7, TILES, 6:7]
            totals[0] = totals[0] + jnp.where(lane == row0 + sub, damp[pl.ds(b, 1)], 0.0)
        for d in range(BAND):
            tiles[b * BAND + d] = totals[d]
        sums[pl.ds(b, 1)] = line

    sums[pl.ds(16, 8)] = blank

    @pl.loop(BLOCK, BLOCK + 7)
    def _(b):
        add_up(b, False)

    ahead = ((block + 1) % N_BLOCKS) * 4 + low
    carry = send(tiles.at[pl.ds(128, 56)], carried, sem.at[2], sem.at[3], ahead, grp)
    carry_sums = send(sums.at[pl.ds(16, 8)], sums_in, sem.at[4], sem.at[5], ahead, grp)

    @pl.loop(0, BLOCK)
    def _(b):
        add_up(b, True)

    carry.wait()
    carry_sums.wait()
    for b in range(7):
        for d in range(7 - b):
            tiles[b * BAND + d] = tiles[b * BAND + d] + carried[b * BAND + d]
    sums[0:8] = sums[0:8] + sums_in[...]
    mine[...] = jnp.broadcast_to(sums[pl.ds(me, 1)], (ROWS, CR))

    @pl.loop(0, 64)
    def _(n):
        fronts[n] = tiles[table[128 + n]]

    for j in range(FRONT):
        fronts[RHS_ITEM, j : j + 1] = sums[pl.ds(table[192 + j], 1)]

    @pl.loop(1, N_BLOCKS)
    def _(step):
        other = (block + step) % N_BLOCKS
        send(fronts.at[pl.ds(2 * other, 2)], spread.at[block], sem.at[6], sem.at[7], other * 4 + low, grp)

    spread[block] = fronts[pl.ds(2 * block, 2)]

    @pl.loop(0, 128)
    def _(o):
        sorted_tiles[o] = tiles[table[o]]

    await_bytes(spread.at[pl.ds(0, N_BLOCKS - 1)], sem.at[7])
    for i in range(2):
        total = spread[0, i]
        for b in range(1, N_BLOCKS):
            total = total + spread[b, i]
        gathered[2 * block + i] = total

    @pl.loop(1, N_BLOCKS)
    def _(step):
        other = (block + step) % N_BLOCKS
        own = gathered.at[pl.ds(2 * block, 2)]
        send(own, own, sem.at[8], sem.at[9], other * 4 + low, grp)

    await_bytes(spread.at[pl.ds(0, N_BLOCKS - 1)], sem.at[9])

    def along_x(begin, count, dst, out, arrive):
        src = gathered.at[pl.ds(begin, count)]
        rows = dst.at[:, pl.ds(row0, ROWS), :]
        pltpu.make_async_copy(src, rows, arrive).start()
        for step in range(1, 4):
            send(src, rows, out, arrive, pts, (grp + step) % 4)

    def along_z(count, dst, out, arrive):
        half = count // 2
        one = dst.at[pl.ds(0, half), pl.ds(row32, 32), :]
        two = dst.at[pl.ds(half, count - half), pl.ds(row32, 32), :]
        return send(one, one, out.at[0], arrive.at[0], above, grp), send(two, two, out.at[1], arrive.at[1], below, grp)

    def to_core(dst, out, arrive):
        half = dst.at[:, pl.ds(row64, 64), :]
        return send(half, half, out, arrive, other_core, grp)

    along_x(0, INNER, inner, sem.at[10], sem.at[11])
    along_x(INNER, OUTER, outer, sem.at[12], sem.at[13])
    await_bytes(inner.at[:, pl.ds(0, 32), :], sem.at[11])
    for copy in along_z(INNER, inner, sem.at[pl.ds(14, 2)], sem.at[pl.ds(16, 2)]):
        copy.wait()
    inner_core = to_core(inner, sem.at[18], sem.at[19])

    to_grp = block // 8
    slot = block % 8

    @pl.loop(0, 128)
    def _(step):
        o = (pts + step) % 128
        here = jnp.logical_and(step == 0, to_grp == grp)
        dst = owned.at[slot, pl.ds(row0, ROWS), :]

        @pl.when(here)
        def _():
            pltpu.make_async_copy(sorted_tiles.at[o], dst, all_sem.at[1]).start()

        @pl.when(jnp.logical_not(here))
        def _():
            send(sorted_tiles.at[o], dst, all_sem.at[0], all_sem.at[1], o, to_grp)

    inner_core.wait()
    for i in range(FRONT):
        for j in range(i, FRONT):
            square[i, j] = inner[INNER_OF[BAND - 1 + i, BAND - 1 + j]]
        inverse[i] = jnp.zeros((CR, FRONT * CR), F32)
    stacked[...] = inner[RHS_ITEM, 0:ROWS]

    row = lax.broadcasted_iota(jnp.int32, (CR, CR), 0)
    col = lax.broadcasted_iota(jnp.int32, (CR, CR), 1)

    def outer_z():
        half = OUTER // 2
        one = outer.at[pl.ds(0, half), pl.ds(row32, 32), :]
        two = outer.at[pl.ds(half, OUTER - half), pl.ds(row32, 32), :]
        pairs = ((one, 0, above), (two, 1, below))
        return [
            pltpu.make_async_remote_copy(
                src_ref=ref,
                dst_ref=ref,
                send_sem=sem.at[25 + n],
                recv_sem=sem.at[27 + n],
                device_id=(to, grp),
                device_id_type=MESH,
            )
            for ref, n, to in pairs
        ]

    def outer_core():
        half = outer.at[:, pl.ds(row64, 64), :]
        return pltpu.make_async_remote_copy(
            src_ref=half,
            dst_ref=half,
            send_sem=sem.at[20],
            recv_sem=sem.at[21],
            device_id=(other_core, grp),
            device_id_type=MESH,
        )

    @pl.loop(0, FRONT)
    def _(k):
        @pl.when(k == 1)
        def _():
            await_bytes(outer.at[:, pl.ds(0, 32), :], sem.at[13])
            for copy in outer_z():
                copy.start()

        @pl.when(k == 3)
        def _():
            for copy in outer_z():
                copy.wait()
            outer_core().start()

        at = pl.multiple_of(CR * k, CR)
        factor_rows(square[k, k], upper.at[0], upper.at[1])
        own = upper[1]
        square[k, k] = jnp.where(row <= col, upper[0], 0.0)
        done = dot_nn(own, inverse[k], PRECISE)
        inverse[k] = done
        inverse[k, :, pl.ds(at, CR)] = own
        for j in range(1, FRONT):

            @pl.when(j > k)
            def _():
                square[k, j] = dot_nn(own, square[k, j], PRECISE)

        for i in range(1, FRONT):

            @pl.when(i > k)
            def _():
                lower = square[k, i]
                inverse[i] = inverse[i] - dot_tn(lower, inverse[k], PRECISE)
                for j in range(i, FRONT):
                    square[i, j] = square[i, j] - dot_tn(lower, square[k, j], PRECISE)

    for j in range(FRONT):

        @pl.when(grp < j)
        def _():
            across_me[j] = square[grp, j].T

        @pl.when(grp == j)
        def _():
            across_me[j] = square[j, j].T

        @pl.when(grp > j)
        def _():
            across_me[j] = jnp.zeros((CR, CR), F32)

    await_bytes(places_in.at[pl.ds(0, BLOCK - 1)], sem.at[22])
    await_bytes(parts.at[pl.ds(0, BLOCK - 1), pl.ds(0, TILES + 1)], sem.at[0])
    await_bytes(spread.at[pl.ds(0, N_BLOCKS - 1)], sem.at[6])
    await_bytes(spread.at[pl.ds(0, N_BLOCKS - 1)], sem.at[8])
    await_bytes(inner.at[:, pl.ds(0, 24), :], sem.at[10])
    await_bytes(outer.at[:, pl.ds(0, 24), :], sem.at[12])

    @pl.when(to_grp == grp)
    def _():
        await_bytes(sorted_tiles.at[pl.ds(0, 127)], all_sem.at[0])

    @pl.when(to_grp != grp)
    def _():
        await_bytes(sorted_tiles, all_sem.at[0])

    await_bytes(owned, all_sem.at[1])
    outer_core().wait()


def factor_rows(block, out_upper, out_inverse):
    count = CR // ROWS
    sub = lax.broadcasted_iota(jnp.int32, (ROWS, CR), 0)
    lane = lax.broadcasted_iota(jnp.int32, (ROWS, CR), 1)
    left = [block[ROWS * s : ROWS * (s + 1)] for s in range(count)]
    right = [jnp.where(sub + ROWS * s == lane, 1.0, 0.0).astype(F32) for s in range(count)]

    def across(value, column):
        return jnp.broadcast_to(value[:, column : column + 1], (ROWS, CR))

    def down(value, row):
        return jnp.broadcast_to(value[row : row + 1], (ROWS, CR))

    for b in range(count):
        base = ROWS * b
        cols = [across(left[b], base + k) for k in range(ROWS)]
        e = [[down(cols[j], i) if j <= i else None for j in range(ROWS)] for i in range(ROWS)]
        x = [down(left[b], i) for i in range(ROWS)]
        y = [down(right[b], i) for i in range(ROWS)]
        inv = []
        for j in range(ROWS):
            scale = lax.rsqrt(e[j][j])
            inv.append(scale)
            for i in range(j + 1, ROWS):
                e[i][j] = e[i][j] * scale
            x[j] = x[j] * scale
            y[j] = y[j] * scale
            for i in range(j + 1, ROWS):
                for k in range(j + 1, i + 1):
                    e[i][k] = e[i][k] - e[i][j] * e[k][j]
                x[i] = x[i] - e[i][j] * x[j]
                y[i] = y[i] - e[i][j] * y[j]
        for j in range(ROWS):
            out_upper[base + j : base + j + 1] = x[j][0:1]
            out_inverse[base + j : base + j + 1] = y[j][0:1]
        if b == count - 1:
            break
        xs = [None] * ROWS
        ys = [None] * ROWS
        for j in reversed(range(ROWS)):
            px, py = x[j], y[j]
            for i in range(j + 1, ROWS):
                px = px - e[i][j] * xs[i]
                py = py - e[i][j] * ys[i]
            xs[j] = px * inv[j]
            ys[j] = py * inv[j]
        for s in range(b + 1, count):
            ratios = [across(left[s], base + k) for k in range(ROWS)]
            for k in range(ROWS):
                left[s] = left[s] - ratios[k] * xs[k]
                right[s] = right[s] - ratios[k] * ys[k]


def front_kernel(
    table, first, owned_hbm, outer, mine, stack, inverse, across_me, tiles_hbm, rhs, panel, rows_of, owned, sem
):
    pts = lax.axis_index("pts")
    grp = lax.axis_index("grp")
    fetch = pltpu.make_async_copy(owned_hbm, owned, sem.at[0])
    fetch.start()
    nil = jnp.zeros((CR, CR), F32)
    lead = BAND - 1

    for i in range(WIN):
        for j in range(FRONT):
            f = lead + j
            if i < lead:
                piece = outer[OUTER_OF[i, f]] if (i, f) in OUTER_OF else nil
            elif i >= lead + FRONT:
                piece = outer[OUTER_OF[f, i]].T if (f, i) in OUTER_OF else nil
            else:
                continue
            rows_of[i, :, CR * j : CR * (j + 1)] = piece

    part = inverse[grp]
    for i in range(WIN):
        if lead <= i < lead + FRONT:
            panel[CR * i : CR * (i + 1)] = across_me[i - lead]
        else:
            panel[CR * i : CR * (i + 1)] = dot_nt(rows_of[i], part, PRECISE)

    base = first[0] + NC - lead
    device = pts * 4 + grp
    stacked = jnp.concatenate([stack[j : j + 1] for j in range(FRONT)], axis=1)
    stacked = jnp.broadcast_to(stacked, (ROWS, FRONT * CR))
    solved = [dot_nt(stacked, inverse[j], PRECISE) for j in range(FRONT)]
    spot = (device + NC - base % NC) % NC
    rhs[...] = mine[0:1]
    for j in range(FRONT):

        @pl.when(spot == lead + j)
        def _():
            rhs[...] = solved[j][0:1]

    in_rest = jnp.logical_and(spot < WIN, jnp.logical_or(spot < lead, spot >= lead + FRONT))

    @pl.when(in_rest)
    def _():
        at = jnp.minimum(spot, WIN - 1)
        total = dot_nn(solved[0], inverse[0], PRECISE)
        for j in range(1, FRONT):
            total = total + dot_nn(solved[j], inverse[j], PRECISE)
        rhs[...] = mine[0:1] - dot_nt(total, rows_of[at], PRECISE)[0:1]

    fetch.wait()
    residue = table[pts]
    ahead = residue % BAND
    near = (residue // BAND + BLOCK - base % BLOCK) % BLOCK
    for extra in range(2):
        one = near + BLOCK * extra
        two = one + ahead
        cluster = (base + one) % NC
        fits = jnp.logical_and(two < WIN, cluster // 128 == grp)
        for p in (one, two):
            fits = jnp.logical_and(fits, jnp.logical_or(p < lead, p >= lead + FRONT))

        @pl.when(fits)
        def _():
            slot = (cluster // BLOCK) % 8
            a = rows_of[jnp.minimum(one, WIN - 1)]
            b = rows_of[jnp.minimum(two, WIN - 1)]
            change = nil
            for j in range(FRONT):
                change = change + dot_nt(dot_nt(a, inverse[j], PRECISE), dot_nt(b, inverse[j], PRECISE), PRECISE)
            owned[slot] = owned[slot] - change

    store = pltpu.make_async_copy(owned, tiles_hbm, sem.at[1])
    store.start()
    store.wait()


def vmem_spec():
    return pl.BlockSpec(memory_space=pltpu.VMEM)


def smem_spec():
    return pl.BlockSpec(memory_space=pltpu.SMEM)


def any_spec():
    return pl.BlockSpec(memory_space=pl.ANY)


def shape(*dims, dtype=F32):
    return jax.ShapeDtypeStruct(dims, dtype)


def per_device(jacobian, point_blocks, point_grad, camera_grad, damping, incidence, tile_owner, front_first):
    block = lax.axis_index("pts") // 4
    jac = jacobian.reshape(TOUCH, CR, COLS)
    damp = lax.dynamic_slice_in_dim(damping, block * BLOCK, BLOCK, 0)
    band, places, table = pl.pallas_call(
        pair_kernel,
        out_shape=(shape(TILES + 1, CR, CR), shape(ROWS, CR, dtype=jnp.int32), shape(256, dtype=jnp.int32)),
        in_specs=[smem_spec()] * 3 + [vmem_spec()] * 4,
        out_specs=(vmem_spec(), vmem_spec(), smem_spec()),
        scratch_shapes=[pltpu.VMEM((TOUCH, CR, COLS), BF16), pltpu.VMEM((TOUCH, CR, COLS), BF16)],
        compiler_params=pltpu.CompilerParams(vmem_limit_bytes=40 * 2**20),
        name="pairs",
    )(
        incidence.reshape(TOUCH),
        tile_owner,
        front_first,
        jac,
        point_blocks.reshape(6, PTS),
        point_grad.reshape(1, COLS),
        camera_grad,
    )
    owned, outer, mine, stack, inverse, across_me = pl.pallas_call(
        exchange_kernel,
        out_shape=(
            shape(8, CR, CR),
            shape(OUTER, CR, CR),
            shape(ROWS, CR),
            shape(ROWS, CR),
            shape(FRONT, CR, FRONT * CR),
            shape(FRONT, CR, CR),
        ),
        in_specs=[smem_spec(), any_spec(), any_spec(), vmem_spec()],
        out_specs=(any_spec(), any_spec(), vmem_spec(), vmem_spec(), vmem_spec(), vmem_spec()),
        scratch_shapes=[
            pltpu.VMEM((30, TILES + 2, ROWS, CR), F32),
            pltpu.VMEM((BLOCK, ROWS, CR), jnp.int32),
            pltpu.VMEM((185, ROWS, CR), F32),
            pltpu.VMEM((56, ROWS, CR), F32),
            pltpu.VMEM((24, CR), F32),
            pltpu.VMEM((ROWS, CR), F32),
            pltpu.VMEM((128, ROWS, CR), F32),
            pltpu.VMEM((64, ROWS, CR), F32),
            pltpu.VMEM((N_BLOCKS, 2, ROWS, CR), F32),
            pltpu.VMEM((64, ROWS, CR), F32),
            pltpu.VMEM((INNER, CR, CR), F32),
            pltpu.VMEM((FRONT, FRONT, CR, CR), F32),
            pltpu.VMEM((2, CR, CR), F32),
            pltpu.SMEM((30, CR), jnp.int32),
            pltpu.SemaphoreType.DMA((32,)),
            pltpu.SemaphoreType.DMA((2,)),
        ],
        compiler_params=pltpu.CompilerParams(
            vmem_limit_bytes=40 * 2**20, has_side_effects=True, collective_id=0
        ),
        name="exchange",
    )(table, band, places, damp)
    return pl.pallas_call(
        front_kernel,
        out_shape=(shape(8, CR, CR), shape(1, CR), shape(WIN * CR, CR)),
        in_specs=[smem_spec(), smem_spec(), any_spec()] + [vmem_spec()] * 5,
        out_specs=(any_spec(), vmem_spec(), vmem_spec()),
        scratch_shapes=[
            pltpu.VMEM((WIN, CR, FRONT * CR), F32),
            pltpu.VMEM((8, CR, CR), F32),
            pltpu.SemaphoreType.DMA((2,)),
        ],
        compiler_params=pltpu.CompilerParams(vmem_limit_bytes=40 * 2**20),
        name="front",
    )(table, front_first, owned, outer, mine, stack, inverse, across_me)


def solution(mesh):
    in_specs = (
        P(("pts", "grp"), None, None, None, None),
        P(("pts", "grp"), None, None),
        P(("pts", "grp"), None, None),
        P(("pts", "grp"), None),
        P(),
        P(("pts", "grp"), None),
        P(),
        P(),
    )
    out_specs = (P(("pts", "grp"), None, None), P(("pts", "grp"), None), P(None, "grp"))
    return jax.shard_map(per_device, mesh=mesh, in_specs=in_specs, out_specs=out_specs, check_vma=False)
```

time: 189 us -> 138 us (0.73); the launches traced: 186 us -> 137 us
  Pallas kernels: 181 us -> 132 us
    pallas_call x1, Pallas kernels: 39.3 us -> 6.47 us  [per_device(): pl.pallas_call(front_kernel, out_shape=(shape(8, CR, CR), shape(1, CR), s...]
    pallas_call x2, Pallas kernels: 142 us -> 126 us  [the longest x1 121 us: per_device(): pl.pallas_call(exchange_kernel, out_shape=(shape(8, CR, CR), shape(OUTER,...]
where the time goes in v2:
time: 138 us; the launch traced here: 137 us
  Pallas kernels  132 us (96%)
  local copies, waits for them, and re-layouts  3.74 us (3%)
  between operations  1.56 us (1%)
    pallas_call x1, Pallas kernels, per_device(): pl.pallas_call(exchange_kernel, out_shape=(shape(8, CR, CR), shape(OUTER,...  121 us
    pallas_call x1, Pallas kernels, per_device(): pl.pallas_call(front_kernel, out_shape=(shape(8, CR, CR), shape(1, CR), s...  6.47 us
    pallas_call x1, Pallas kernels, per_device(): pl.pallas_call(pair_kernel, out_shape=(shape(TILES + 1, CR, CR), shape(RO...  4.48 us
    unnamed x11, local copies, waits for them, and re-layouts  3.13 us

profile of v2, /device:TPU:1, one launch (start us, length us, event | category | flops | bytes accessed | tf_op | source)
XLA Modules:
  0.0 137.4 jit_solution(11342121529310410729)
XLA Ops:
  0.6 0.0 copy-start
  1.4 0.7 copy.15
  2.0 0.0 copy-done
  2.0 0.7 copy.17
  2.7 1.7 %copy.12 = bf16[1,6,128,3,256]{2,4,3,1,0:T(8,128)(2,1)S(1)} copy(bf16[1,6,128,3,256]{4,2,3,1,0:T(8,128)(2,1)} %param.8) | data formatting | bytes 2359296 | tf_op args[0]
  4.4 0.0 copy-start.1
  4.4 0.0 copy-start.2
  4.5 0.0 copy-start.3
  4.5 0.6 copy.13.jac
  5.1 0.0 copy-done.1
  5.1 0.0 copy-done.2
  5.1 0.0 copy-done.3
  5.1 4.5 %pairs.1 = (f32[22,128,128]{2,1,0:T(8,128)S(1)}, s32[8,128]{1,0:T(8,128)S(1)}, s32[256]{0:T(256)S(1)}) custom-call(s32[6]{0:T(128)S(1)} %bitcast.9, s32[128]{0:T(128)S(1)} %copy-done.2, s32[1]{0:T(128)S(6)} %copy.18.first, bf16[6,128,768]{2,1,0:T(8,128)(2,1)S(1)} %copy.13.jac, f32[6,256]{1,0:T(8,128)S(1)} %bitcast.7, bf16[1,768]{1,0:T(2,128)(2,1)S(1)} %bitcast.8, ...), custom_call_target="tpu_custom_call" | custom-call | tf_op jit(solution)/shard_map/pairs/pallas_call | solution.py:605
  9.6 121.1 %exchange.1 = (f32[8,128,128]{2,1,0:T(8,128)S(1)}, f32[44,128,128]{2,1,0:T(8,128)S(1)}, f32[8,128]{1,0:T(8,128)S(1)}, f32[8,128]{1,0:T(8,128)S(1)}, f32[4,128,51...) custom-call(s32[256]{0:T(256)S(1)} %get-tuple-element.12.table, f32[22,128,128]{2,1,0:T(8,128)S(1)} %get-tuple-element.13.band, ...), custom_call_target="tpu_custom_call" | custom-call | tf_op jit(solution)/shard_map/exchange/pallas_call | solution.py:622
  130.8 6.5 %front.1 = (f32[8,128,128]{2,1,0:T(8,128)}, f32[1,128]{1,0:T(1,128)}, f32[2304,128]{1,0:T(8,128)}) custom-call(s32[256]{0:T(256)S(1)} %get-tuple-element.12.table, s32[1]{0:T(128)S(6)} %copy.18.first, f32[8,128,128]{2,1,0:T(8,128)S(1)} %get-tuple-element.15.owned_hbm, f32[44,128,128]{2,1,0:T(8,128)S(1)} %get-tuple-element.16.outer, ...), custom_call_target="tpu_custom_call" | custom-call | tf_op jit(solution)/shard_map/front/pallas_call | solution.py:657
  (1 shorter events, 0.0 us)
Async XLA Ops:
  0.6 1.4 %copy-start = (f32[512,128]{1,0:T(8,128)S(1)}, f32[512,128]{1,0:T(8,128)}, u32[]{:S(2)}) copy-start(f32[512,128]{1,0:T(8,128)} %param.12) | copy-start | bytes 786436
  4.4 0.7 copy-start.1
  4.4 0.7 copy-start.2
  4.5 0.7 copy-start.3

commit v3 on v2

v3 whole, which is shorter than its diff:
```python
import jax
import jax.numpy as jnp
from jax import lax
from jax.experimental import pallas as pl
from jax.experimental.pallas import tpu as pltpu
from jax.sharding import PartitionSpec as P

TOUCH = 6
BAND = 8
FRONT = 4
CR = 128
PTS = 256
COLS = 3 * PTS
NC = 512
WIN = 18
BLOCK = 16
N_BLOCKS = 32
ROWS = 8
TILES = 21
NONE = 64
INNER = 11
OUTER = 44
EARLY = 28
MESH = pl.DeviceIdType.MESH
PRECISE = lax.Precision.HIGHEST
F32 = jnp.float32
BF16 = jnp.bfloat16


def tile_index(i, j):
    return (TOUCH - 1) * i - i * (i - 1) // 2 + j


def front_items():
    first = BAND - 1
    last = first + FRONT
    inside = [(i, j) for i in range(first, last) for j in range(i, last)]
    before = [(i, j) for i in range(first) for j in range(first, last) if j - i < BAND]
    after = [(i, j) for i in range(first, last) for j in range(last, WIN) if j - i < BAND]
    return inside + before + after


FRONT_ITEMS = front_items()
RHS_ITEM = 10
OUTER_OF = {pair: n - 10 for n, pair in enumerate(FRONT_ITEMS) if n >= 10}
INNER_OF = {pair: n for n, pair in enumerate(FRONT_ITEMS) if n < 10}
PLACES, PARTS, CARRY, CARRY_SUMS, SPREAD_IN, GATHER_IN, SPREAD_OUT, GATHER_OUT = range(8)
INNER_X, INNER_CORE, OUTER_X, OUTER_CORE, OWNED, SPARE, SPOTS = range(8, 15)
INNER_Z = 15
OUTER_Z = 18
FETCH = 21
OUTER_Z2 = 27
OUTER_X2 = 30
FIRST_X = 28
LINKS = 31
ZERO_TILE = 184
ZERO_ROW = 23


def dot_nt(a, b, precision=None):
    return lax.dot_general(a, b, (((1,), (1,)), ((), ())), precision=precision, preferred_element_type=F32)


def dot_three(a, b):
    a_high, b_high = a.astype(BF16), b.astype(BF16)
    a_low = (a - a_high.astype(F32)).astype(BF16)
    b_low = (b - b_high.astype(F32)).astype(BF16)
    return dot_nt(a_high, b_high) + (dot_nt(a_high, b_low) + dot_nt(a_low, b_high))


def dot_nn(a, b, precision=None):
    return lax.dot_general(a, b, (((1,), (0,)), ((), ())), precision=precision, preferred_element_type=F32)


def dot_tn(a, b, precision=None):
    return lax.dot_general(a, b, (((0,), (0,)), ((), ())), precision=precision, preferred_element_type=F32)


def invert_blocks(blocks):
    diag_x, diag_y, diag_z = blocks[0:1], blocks[1:2], blocks[2:3]
    cross_xy, cross_xz, cross_yz = blocks[3:4], blocks[4:5], blocks[5:6]
    adj_xx = diag_y * diag_z - cross_yz * cross_yz
    adj_yy = diag_x * diag_z - cross_xz * cross_xz
    adj_zz = diag_x * diag_y - cross_xy * cross_xy
    adj_xy = cross_xz * cross_yz - cross_xy * diag_z
    adj_xz = cross_xy * cross_yz - diag_y * cross_xz
    adj_yz = cross_xy * cross_xz - diag_x * cross_yz
    determinant = diag_x * adj_xx + cross_xy * adj_xy + cross_xz * adj_xz
    inverse_det = 1.0 / determinant
    return [
        [adj_xx * inverse_det, adj_xy * inverse_det, adj_xz * inverse_det],
        [adj_xy * inverse_det, adj_yy * inverse_det, adj_yz * inverse_det],
        [adj_xz * inverse_det, adj_yz * inverse_det, adj_zz * inverse_det],
    ]


def exchange_kernel(
    owners,
    first,
    inc_hbm,
    jac_hbm,
    blocks_hbm,
    grad_hbm,
    cam_hbm,
    damping,
    owned,
    outer,
    mine,
    stacked,
    inverse,
    across_me,
    jac_sorted,
    scl_sorted,
    band,
    places,
    damp,
    parts,
    places_in,
    tiles,
    carried,
    sums,
    sums_in,
    sorted_tiles,
    fronts_in,
    fronts_out,
    spread_in,
    spread_out,
    gathered_in,
    gathered_out,
    inner,
    square,
    upper,
    mine_out,
    jac,
    blocks,
    grad,
    cam,
    inc,
    spots,
    sem,
):
    pts = lax.axis_index("pts")
    grp = lax.axis_index("grp")
    device = pts * 4 + grp
    block = pts // 4
    low = pts % 4
    core = low % 2
    depth = low // 2
    me = 4 * low + grp
    my_rows = core * 8 + grp * 2 + depth
    row0 = pl.multiple_of(ROWS * my_rows, ROWS)
    row16 = pl.multiple_of(core * 64 + grp * 16, 16)
    row64 = pl.multiple_of(core * 64, 64)
    z = (pts // 2) % 8
    above = pts - 2 * z + 2 * ((z + 1) % 8)
    below = pts - 2 * z + 2 * ((z + 7) % 8)
    other_core = pts + 1 - 2 * core
    home = (11 * block) % N_BLOCKS
    home_in = home < INNER
    home_out = home < OUTER // 2

    def link(src, dst, which, to_pts, to_grp):
        return pltpu.make_async_remote_copy(
            src_ref=src,
            dst_ref=dst,
            send_sem=sem.at[2 * which],
            recv_sem=sem.at[2 * which + 1],
            device_id=(to_pts, to_grp),
            device_id_type=MESH,
        )

    def local(src, dst, which):
        return pltpu.make_async_copy(src, dst, sem.at[2 * which + 1])

    def sent(ref, which):
        pltpu.make_async_copy(ref, ref, sem.at[2 * which]).wait()

    def arrived(ref, which):
        pltpu.make_async_copy(ref, ref, sem.at[2 * which + 1]).wait()

    fetches = [
        local(inc_hbm, inc, FETCH),
        local(jac_hbm, jac, FETCH + 1),
        local(blocks_hbm, blocks, FETCH + 2),
        local(grad_hbm, grad, FETCH + 3),
        local(cam_hbm, cam, FETCH + 4),
        local(damping.at[pl.ds(pl.multiple_of(BLOCK * block, BLOCK), BLOCK)], damp, FETCH + 5),
    ]
    for fetch in fetches:
        fetch.start()

    barrier = pltpu.get_barrier_semaphore()

    @pl.loop(1, BLOCK)
    def _(step):
        peer = (me + step) % BLOCK
        pl.semaphore_signal(barrier, inc=1, device_id=(block * 4 + peer // 4, peer % 4), device_id_type=MESH)

    @pl.loop(1, N_BLOCKS)
    def _(step):
        other = (block + step) % N_BLOCKS
        pl.semaphore_signal(barrier, inc=1, device_id=(other * 4 + low, grp), device_id_type=MESH)

    for fetch in fetches:
        fetch.wait()

    sub = lax.broadcasted_iota(jnp.int32, (ROWS, CR), 0)
    lane = lax.broadcasted_iota(jnp.int32, (ROWS, CR), 1)
    slots = [(inc[0, k] + NC - device) % NC for k in range(TOUCH)]
    order = [jnp.int32(0)] * TOUCH
    place = jnp.full((ROWS, CR), NONE, jnp.int32)
    for k in range(TOUCH):
        rank = jnp.int32(0)
        for other in range(TOUCH):
            if other != k:
                rank = rank + (slots[other] < slots[k]).astype(jnp.int32)
        order = [order[r] + jnp.where(rank == r, k, 0) for r in range(TOUCH)]
        place = jnp.where(lane == slots[k], tile_index(rank, 0), place)
        place = jnp.where(lane == slots[k] + BAND, rank, place)
    places[...] = place

    factors = invert_blocks(jnp.concatenate([blocks[k] for k in range(6)], axis=0))
    for r in range(TOUCH):
        wide = []
        for c in range(3):
            piece = jac[jnp.minimum(order[r], TOUCH - 1), c]
            jac_sorted[r, :, PTS * c : PTS * (c + 1)] = piece
            wide.append(piece.astype(F32))
        for c in range(3):
            summed = wide[0] * factors[0][c]
            summed = summed + wide[1] * factors[1][c]
            summed = summed + wide[2] * factors[2][c]
            scl_sorted[r, :, PTS * c : PTS * (c + 1)] = summed.astype(BF16)

    blank = jnp.zeros((ROWS, CR), F32)

    def send_group(begin, count):
        @pl.loop(1, BLOCK)
        def _(step):
            peer = (me + step) % BLOCK
            p_low = peer // 4
            p_grp = peer % 4
            rows = pl.multiple_of(ROWS * ((p_low % 2) * 8 + p_grp * 2 + p_low // 2), ROWS)
            if begin == 0:
                link(places, places_in.at[me], PLACES, block * 4 + p_low, p_grp).start()
            src = band.at[pl.ds(begin, count), pl.ds(rows, ROWS), :]
            link(src, parts.at[7 + me, pl.ds(begin, count)], PARTS, block * 4 + p_low, p_grp).start()

        local(
            band.at[pl.ds(begin, count), pl.ds(row0, ROWS), :], parts.at[7 + me, pl.ds(begin, count)], PARTS
        ).start()

    for i in range(TOUCH):
        for j in range(i, TOUCH):
            band[tile_index(i, j)] = dot_nt(scl_sorted[i], jac_sorted[j])
        if i == 0:
            local(places, places_in.at[me], PLACES).start()
            pl.semaphore_wait(barrier, BLOCK - 1 + N_BLOCKS - 1)
            send_group(0, 6)
        if i == 1:
            send_group(6, 5)
    grad16 = [jnp.broadcast_to(grad[c : c + 1], (16, PTS)) for c in range(3)]
    grad16 = jnp.concatenate(grad16, axis=1)
    rows = [-dot_nt(grad16, scl_sorted[i])[0:1] for i in range(TOUCH)]
    chunk = jnp.concatenate([*rows, cam[...], jnp.zeros((1, CR), F32)], axis=0)
    for j in range(16):
        band[TILES, ROWS * j : ROWS * (j + 1)] = chunk
    send_group(11, TILES + 1 - 11)

    @pl.loop(0, 30)
    def _(q):
        parts[q, TILES + 1] = blank

    for q in (*range(7), *range(23, 30)):
        parts[q, TILES] = blank

        @pl.loop(0, 2 * BAND)
        def _(n):
            spots[q, n] = NONE

    tiles[ZERO_TILE] = blank
    sums[pl.ds(16, 8)] = blank
    arrived(places_in, PLACES)
    to_scalars = local(places_in.at[:, 0, :], spots.at[pl.ds(7, BLOCK)], SPOTS)
    to_scalars.start()
    to_scalars.wait()
    arrived(parts.at[pl.ds(7, BLOCK), pl.ds(0, TILES + 1)], PARTS)

    def add_up(b, own):
        totals = [None] * BAND
        line = None
        for a in range(BAND):
            q = b - a + 7
            here = spots[q, a]
            for d in range(BAND - a):
                value = parts[q, jnp.minimum(here + spots[q, BAND + a + d], TILES + 1)]
                totals[d] = value if totals[d] is None else totals[d] + value
            row = parts[q, TILES, pl.ds(jnp.minimum(spots[q, BAND + a], 7), 1)]
            line = row if line is None else line + row
        if own:
            line = line + parts[b + 7, TILES, 6:7]
            totals[0] = totals[0] + jnp.where(lane == row0 + sub, damp[pl.ds(b, 1)], 0.0)
        for d in range(BAND):
            tiles[b * BAND + d] = totals[d]
        sums[pl.ds(b, 1)] = line

    @pl.loop(BLOCK, BLOCK + 7)
    def _(b):
        add_up(b, False)

    ahead = ((block + 1) % N_BLOCKS) * 4 + low
    for b in range(7):
        src = tiles.at[pl.ds((BLOCK + b) * BAND, 7 - b)]
        link(src, carried.at[pl.ds(b * BAND, 7 - b)], CARRY, ahead, grp).start()
    carry_sums = link(sums.at[pl.ds(16, 8)], sums_in, CARRY_SUMS, ahead, grp)
    carry_sums.start()

    @pl.loop(0, BLOCK)
    def _(b):
        add_up(b, True)

    arrived(carried.at[pl.ds(0, 28)], CARRY)
    carry_sums.wait()
    for b in range(7):
        for d in range(7 - b):
            tiles[b * BAND + d] = tiles[b * BAND + d] + carried[b * BAND + d]
    sums[0:8] = sums[0:8] + sums_in[...]
    mine[...] = jnp.broadcast_to(sums[pl.ds(me, 1)], (ROWS, CR))

    window = first[0] + NC - (BAND - 1)

    def spot_of(pair):
        cluster = (window + pair[0]) % NC
        spot = (cluster % BLOCK) * BAND + (pair[1] - pair[0])
        return jnp.where(cluster // BLOCK == block, spot, ZERO_TILE)

    for n in range(RHS_ITEM):
        fronts_in[n] = tiles[spot_of(FRONT_ITEMS[n])]
    fronts_in[RHS_ITEM] = blank
    for j in range(FRONT):
        cluster = (first[0] + j) % NC
        spot = jnp.where(cluster // BLOCK == block, cluster % BLOCK, ZERO_ROW)
        fronts_in[RHS_ITEM, j : j + 1] = sums[pl.ds(spot, 1)]

    @pl.loop(1, INNER + 1)
    def _(step):
        n = (home + step) % INNER
        to = (3 * n) % N_BLOCKS

        @pl.when(to != block)
        def _():
            link(fronts_in.at[n], spread_in.at[block], SPREAD_IN, to * 4 + low, grp).start()

    for n in range(OUTER):
        fronts_out[n] = tiles[spot_of(FRONT_ITEMS[n + 10])]

    @pl.loop(1, OUTER // 2 + 1)
    def _(step):
        n = (home + step) % (OUTER // 2)
        to = (3 * n) % N_BLOCKS

        @pl.when(to != block)
        def _():
            link(fronts_out.at[pl.ds(2 * n, 2)], spread_out.at[block], SPREAD_OUT, to * 4 + low, grp).start()

    @pl.when(home_in)
    def _():
        spread_in[block] = fronts_in[home]
        arrived(spread_in.at[pl.ds(0, N_BLOCKS - 1)], SPREAD_IN)
        total = spread_in[0]
        for b in range(1, N_BLOCKS):
            total = total + spread_in[b]
        gathered_in[home] = total

        @pl.loop(1, N_BLOCKS)
        def _(step):
            other = (block + step) % N_BLOCKS
            link(gathered_in.at[home], gathered_in.at[home], GATHER_IN, other * 4 + low, grp).start()

    @pl.loop(0, 128)
    def _(o):
        sorted_tiles[o] = tiles[owners[o]]

    @pl.when(home_in)
    def _():
        arrived(gathered_in.at[pl.ds(0, INNER - 1)], GATHER_IN)

    @pl.when(jnp.logical_not(home_in))
    def _():
        arrived(gathered_in, GATHER_IN)

    def along_z(src, dst, count, which):
        half = count // 2
        one = link(src.at[pl.ds(0, half)], dst.at[pl.ds(0, half)], which, above, grp)
        two = link(src.at[pl.ds(half, count - half)], dst.at[pl.ds(half, count - half)], which + 1, below, grp)
        return one, two

    def along_x(src, dst, which):
        return [link(src, dst, which, pts, (grp + step) % 4) for step in range(1, 4)]

    def start(*copies):
        for copy in copies:
            copy.start()

    def wait(*copies):
        for copy in copies:
            copy.wait()

    def same(ref, which, to_pts):
        return link(ref, ref, which, to_pts, grp)

    inner_rows = inner.at[:, core, grp, depth]
    inner_z = (*along_z(gathered_in, inner_rows, INNER, INNER_Z), local(gathered_in, inner_rows, INNER_Z + 2))
    start(*inner_z)

    @pl.when(home_out)
    def _():
        spread_out[block] = fronts_out[pl.ds(2 * home, 2)]
        arrived(spread_out.at[pl.ds(0, N_BLOCKS - 1)], SPREAD_OUT)
        for i in range(2):
            total = spread_out[0, i]
            for b in range(1, N_BLOCKS):
                total = total + spread_out[b, i]
            mine_out[i] = total
        local(mine_out, gathered_out.at[pl.ds(2 * home, 2)], GATHER_OUT).start()

        @pl.loop(1, N_BLOCKS)
        def _(step):
            other = (block + step) % N_BLOCKS
            link(mine_out, gathered_out.at[pl.ds(2 * home, 2)], GATHER_OUT, other * 4 + low, grp).start()

    wait(*inner_z)
    inner_pair = inner.at[:, core, grp]
    start(*along_x(inner_pair, inner_pair, INNER_X))
    arrived(inner.at[:, 0, pl.ds(0, 3)], INNER_X)
    inner_core = same(inner.at[:, core], INNER_CORE, other_core)
    inner_core.start()

    first_rows = outer.at[pl.ds(0, EARLY), core, grp, depth]
    first_four = outer.at[pl.ds(0, EARLY), core, :, depth]
    other_rows = outer.at[pl.ds(EARLY, OUTER - EARLY), core, grp, depth]
    other_pair = outer.at[pl.ds(EARLY, OUTER - EARLY), core, grp]
    first_src = gathered_out.at[pl.ds(0, EARLY)]
    other_src = gathered_out.at[pl.ds(EARLY, OUTER - EARLY)]
    first_x = along_x(first_src, first_rows, OUTER_X)
    other_z = along_z(other_src, other_rows, OUTER - EARLY, OUTER_Z)
    own_rows = (local(first_src, first_rows, OUTER_X2), local(other_src, other_rows, OUTER_Z + 2))
    first_z = along_z(first_four, first_four, EARLY, OUTER_Z2)
    other_x = along_x(other_pair, other_pair, FIRST_X + 1)
    outer_core = same(outer.at[:, core], OUTER_CORE, other_core)

    def phase_one():
        arrived(gathered_out, GATHER_OUT)
        start(*first_x, *other_z, *own_rows)

    def phase_two():
        wait(*own_rows, *other_z)
        arrived(outer.at[pl.ds(0, EARLY), 0, pl.ds(0, 3), 0], OUTER_X)
        start(*first_z, *other_x)

    def phase_three():
        wait(*first_z)
        arrived(outer.at[pl.ds(EARLY, OUTER - EARLY), 0, pl.ds(0, 3)], FIRST_X + 1)
        outer_core.start()

    to_grp = block // 8
    slot = block % 8

    @pl.loop(0, 128)
    def _(step):
        o = (pts + step) % 128
        here = jnp.logical_and(step == 0, to_grp == grp)
        dst = owned.at[slot, pl.ds(row0, ROWS), :]

        @pl.when(here)
        def _():
            local(sorted_tiles.at[o], dst, OWNED).start()

        @pl.when(jnp.logical_not(here))
        def _():
            link(sorted_tiles.at[o], dst, OWNED, o, to_grp).start()

    inner_core.wait()
    for i in range(FRONT):
        for j in range(i, FRONT):
            square[i, j] = inner[INNER_OF[BAND - 1 + i, BAND - 1 + j]].reshape(CR, CR)
        for j in range(i + 1, FRONT):
            inverse[i, :, CR * j : CR * (j + 1)] = jnp.zeros((CR, CR), F32)
    stacked[...] = inner[RHS_ITEM, 0, 0, 0]

    row = lax.broadcasted_iota(jnp.int32, (CR, CR), 0)
    col = lax.broadcasted_iota(jnp.int32, (CR, CR), 1)

    def at(j):
        return slice(CR * j, CR * (j + 1))

    hooks = [{8: phase_one}, {8: phase_two}, {8: phase_three}, {}]
    for k in range(FRONT):
        factor_rows(square[k, k], upper.at[2 * k], upper.at[2 * k + 1], hooks[k])
        own = upper[2 * k + 1]
        square[k, k] = jnp.where(row <= col, upper[2 * k], 0.0)
        for j in range(k + 1, FRONT):
            square[k, j] = dot_nn(own, square[k, j], PRECISE)
        for i in range(k + 1, FRONT):
            for j in range(i, FRONT):
                square[i, j] = square[i, j] - dot_tn(square[k, i], square[k, j], PRECISE)
        for j in range(k):
            inverse[k, :, at(j)] = dot_nn(own, inverse[k, :, at(j)], PRECISE)
        inverse[k, :, at(k)] = own
        for i in range(k + 1, FRONT):
            for j in range(k + 1):
                change = dot_tn(square[k, i], inverse[k, :, at(j)], PRECISE)
                inverse[i, :, at(j)] = -change if j == k else inverse[i, :, at(j)] - change

    for j in range(FRONT):

        @pl.when(grp < j)
        def _():
            across_me[j] = square[grp, j].T

        @pl.when(grp == j)
        def _():
            across_me[j] = square[j, j].T

        @pl.when(grp > j)
        def _():
            across_me[j] = jnp.zeros((CR, CR), F32)

    sent(places_in.at[pl.ds(0, BLOCK - 1)], PLACES)
    sent(parts.at[pl.ds(0, BLOCK - 1), pl.ds(0, TILES + 1)], PARTS)
    sent(carried.at[pl.ds(0, 28)], CARRY)
    sent(inner.at[:, 0, pl.ds(0, 3)], INNER_X)
    sent(outer.at[pl.ds(0, EARLY), 0, pl.ds(0, 3), 0], OUTER_X)
    sent(outer.at[pl.ds(EARLY, OUTER - EARLY), 0, pl.ds(0, 3)], FIRST_X + 1)

    @pl.when(home_in)
    def _():
        sent(gathered_in.at[pl.ds(0, INNER - 1)], SPREAD_IN)
        sent(spread_in.at[pl.ds(0, N_BLOCKS - 1)], GATHER_IN)

    @pl.when(jnp.logical_not(home_in))
    def _():
        sent(gathered_in, SPREAD_IN)

    @pl.when(home_out)
    def _():
        sent(gathered_out.at[pl.ds(0, OUTER - 2)], SPREAD_OUT)
        sent(spread_out.at[pl.ds(0, N_BLOCKS - 1)], GATHER_OUT)

    @pl.when(jnp.logical_not(home_out))
    def _():
        sent(gathered_out, SPREAD_OUT)

    @pl.when(to_grp == grp)
    def _():
        sent(sorted_tiles.at[pl.ds(0, 127)], OWNED)

    @pl.when(to_grp != grp)
    def _():
        sent(sorted_tiles, OWNED)

    arrived(owned, OWNED)
    outer_core.wait()


def factor_rows(block, out_upper, out_inverse, hooks):
    count = CR // ROWS
    sub = lax.broadcasted_iota(jnp.int32, (ROWS, CR), 0)
    lane = lax.broadcasted_iota(jnp.int32, (ROWS, CR), 1)
    left = [block[ROWS * s : ROWS * (s + 1)] for s in range(count)]
    right = [jnp.where(sub + ROWS * s == lane, 1.0, 0.0).astype(F32) for s in range(count)]

    def across(value, column):
        return jnp.broadcast_to(value[:, column : column + 1], (ROWS, CR))

    def down(value, row):
        return jnp.broadcast_to(value[row : row + 1], (ROWS, CR))

    for b in range(count):
        if b in hooks:
            hooks[b]()
        base = ROWS * b
        cols = [across(left[b], base + k) for k in range(ROWS)]
        e = [[down(cols[j], i) if j <= i else None for j in range(ROWS)] for i in range(ROWS)]
        x = [down(left[b], i) for i in range(ROWS)]
        y = [down(right[b], i) for i in range(ROWS)]
        inv = []
        for j in range(ROWS):
            scale = lax.rsqrt(e[j][j])
            inv.append(scale)
            for i in range(j + 1, ROWS):
                e[i][j] = e[i][j] * scale
            x[j] = x[j] * scale
            y[j] = y[j] * scale
            for i in range(j + 1, ROWS):
                for k in range(j + 1, i + 1):
                    e[i][k] = e[i][k] - e[i][j] * e[k][j]
                x[i] = x[i] - e[i][j] * x[j]
                y[i] = y[i] - e[i][j] * y[j]
        for j in range(ROWS):
            out_upper[base + j : base + j + 1] = x[j][0:1]
            out_inverse[base + j : base + j + 1] = y[j][0:1]
        if b == count - 1:
            break
        xs = [None] * ROWS
        ys = [None] * ROWS
        for j in reversed(range(ROWS)):
            px, py = x[j], y[j]
            for i in range(j + 1, ROWS):
                px = px - e[i][j] * xs[i]
                py = py - e[i][j] * ys[i]
            xs[j] = px * inv[j]
            ys[j] = py * inv[j]
        for s in range(b + 1, count):
            ratios = [across(left[s], base + k) for k in range(ROWS)]
            for k in range(ROWS):
                left[s] = left[s] - ratios[k] * xs[k]
                right[s] = right[s] - ratios[k] * ys[k]


def front_kernel(
    owners,
    first,
    owned_hbm,
    outer_hbm,
    mine_hbm,
    stack_hbm,
    inverse_hbm,
    across_hbm,
    tiles_hbm,
    rhs,
    panel,
    rows_of,
    owned,
    outer,
    mine,
    stack,
    inverse,
    across_me,
    sem,
):
    pts = lax.axis_index("pts")
    grp = lax.axis_index("grp")
    fetch = pltpu.make_async_copy(owned_hbm, owned, sem.at[0])
    pairs = ((outer_hbm, outer), (inverse_hbm, inverse), (across_hbm, across_me), (mine_hbm, mine), (stack_hbm, stack))
    fetches = [pltpu.make_async_copy(src, dst, sem.at[2 + n]) for n, (src, dst) in enumerate(pairs)]
    for copy in fetches:
        copy.start()
    fetch.start()
    for copy in fetches:
        copy.wait()
    nil = jnp.zeros((CR, CR), F32)
    lead = BAND - 1

    for i in range(WIN):
        for j in range(FRONT):
            f = lead + j
            if i < lead:
                piece = outer[OUTER_OF[i, f]] if (i, f) in OUTER_OF else nil
            elif i >= lead + FRONT:
                piece = outer[OUTER_OF[f, i]].T if (f, i) in OUTER_OF else nil
            else:
                continue
            rows_of[i, :, CR * j : CR * (j + 1)] = piece

    part = inverse[grp]
    for i in range(WIN):
        if lead <= i < lead + FRONT:
            panel[CR * i : CR * (i + 1)] = across_me[i - lead]
        else:
            panel[CR * i : CR * (i + 1)] = dot_three(rows_of[i], part)

    base = first[0] + NC - lead
    device = pts * 4 + grp
    stacked = jnp.concatenate([stack[j : j + 1] for j in range(FRONT)], axis=1)
    stacked = jnp.broadcast_to(stacked, (ROWS, FRONT * CR))
    solved = [dot_nt(stacked, inverse[j], PRECISE) for j in range(FRONT)]
    spot = (device + NC - base % NC) % NC
    rhs[...] = mine[0:1]
    for j in range(FRONT):

        @pl.when(spot == lead + j)
        def _():
            rhs[...] = solved[j][0:1]

    in_rest = jnp.logical_and(spot < WIN, jnp.logical_or(spot < lead, spot >= lead + FRONT))

    @pl.when(in_rest)
    def _():
        at = jnp.minimum(spot, WIN - 1)
        total = dot_nn(solved[0], inverse[0], PRECISE)
        for j in range(1, FRONT):
            total = total + dot_nn(solved[j], inverse[j], PRECISE)
        rhs[...] = mine[0:1] - dot_nt(total, rows_of[at], PRECISE)[0:1]

    fetch.wait()
    residue = owners[pts]
    ahead = residue % BAND
    near = (residue // BAND + BLOCK - base % BLOCK) % BLOCK
    for extra in range(2):
        one = near + BLOCK * extra
        two = one + ahead
        cluster = (base + one) % NC
        fits = jnp.logical_and(two < WIN, cluster // 128 == grp)
        for p in (one, two):
            fits = jnp.logical_and(fits, jnp.logical_or(p < lead, p >= lead + FRONT))

        @pl.when(fits)
        def _():
            slot = (cluster // BLOCK) % 8
            a = rows_of[jnp.minimum(one, WIN - 1)]
            b = rows_of[jnp.minimum(two, WIN - 1)]
            change = nil
            for j in range(FRONT):
                deep = CR * (j + 1)
                row = inverse[j, :, :deep]
                change = change + dot_three(dot_three(a[:, :deep], row), dot_three(b[:, :deep], row))
            owned[slot] = owned[slot] - change

    store = pltpu.make_async_copy(owned, tiles_hbm, sem.at[1])
    store.start()
    store.wait()


def vmem_spec():
    return pl.BlockSpec(memory_space=pltpu.VMEM)


def smem_spec():
    return pl.BlockSpec(memory_space=pltpu.SMEM)


def any_spec():
    return pl.BlockSpec(memory_space=pl.ANY)


def shape(*dims, dtype=F32):
    return jax.ShapeDtypeStruct(dims, dtype)


def per_device(jacobian, point_blocks, point_grad, camera_grad, damping, incidence, tile_owner, front_first):
    index = jnp.arange(128, dtype=jnp.int32)
    owners = jnp.sum(jnp.where(tile_owner[:, None] == index[None, :], index[:, None], 0), axis=0)
    owned, outer, mine, stack, inverse, across_me = pl.pallas_call(
        exchange_kernel,
        out_shape=(
            shape(8, CR, CR),
            shape(OUTER, 2, 4, 2, ROWS, CR),
            shape(ROWS, CR),
            shape(ROWS, CR),
            shape(FRONT, CR, FRONT * CR),
            shape(FRONT, CR, CR),
        ),
        in_specs=[smem_spec()] * 2 + [pl.BlockSpec(memory_space=pltpu.HBM)] * 6,
        out_specs=(any_spec(), any_spec(), vmem_spec(), vmem_spec(), vmem_spec(), vmem_spec()),
        scratch_shapes=[
            pltpu.VMEM((TOUCH, CR, COLS), BF16),
            pltpu.VMEM((TOUCH, CR, COLS), BF16),
            pltpu.VMEM((TILES + 1, CR, CR), F32),
            pltpu.VMEM((ROWS, CR), jnp.int32),
            pltpu.VMEM((BLOCK, CR), F32),
            pltpu.VMEM((30, TILES + 2, ROWS, CR), F32),
            pltpu.VMEM((BLOCK, ROWS, CR), jnp.int32),
            pltpu.VMEM((185, ROWS, CR), F32),
            pltpu.VMEM((56, ROWS, CR), F32),
            pltpu.VMEM((24, CR), F32),
            pltpu.VMEM((ROWS, CR), F32),
            pltpu.VMEM((128, ROWS, CR), F32),
            pltpu.VMEM((INNER, ROWS, CR), F32),
            pltpu.VMEM((OUTER, ROWS, CR), F32),
            pltpu.VMEM((N_BLOCKS, ROWS, CR), F32),
            pltpu.VMEM((N_BLOCKS, 2, ROWS, CR), F32),
            pltpu.VMEM((INNER, ROWS, CR), F32),
            pltpu.VMEM((OUTER, ROWS, CR), F32),
            pltpu.VMEM((INNER, 2, 4, 2, ROWS, CR), F32),
            pltpu.VMEM((FRONT, FRONT, CR, CR), F32),
            pltpu.VMEM((2 * FRONT, CR, CR), F32),
            pltpu.VMEM((2, ROWS, CR), F32),
            pltpu.VMEM((TOUCH, 3, CR, PTS), BF16),
            pltpu.VMEM((6, 1, PTS), F32),
            pltpu.VMEM((3, PTS), BF16),
            pltpu.VMEM((1, CR), F32),
            pltpu.SMEM((1, TOUCH), jnp.int32),
            pltpu.SMEM((30, CR), jnp.int32),
            pltpu.SemaphoreType.DMA((2 * LINKS,)),
        ],
        compiler_params=pltpu.CompilerParams(
            vmem_limit_bytes=60 * 2**20, has_side_effects=True, collective_id=0
        ),
        name="exchange",
    )(
        owners,
        front_first,
        incidence,
        jacobian.reshape(TOUCH, CR, 3, PTS).transpose(0, 2, 1, 3),
        point_blocks.transpose(1, 0, 2),
        point_grad.reshape(3, PTS),
        camera_grad,
        damping,
    )
    return pl.pallas_call(
        front_kernel,
        out_shape=(shape(8, CR, CR), shape(1, CR), shape(WIN * CR, CR)),
        in_specs=[smem_spec()] * 2 + [pl.BlockSpec(memory_space=pltpu.HBM)] * 6,
        out_specs=(any_spec(), vmem_spec(), vmem_spec()),
        scratch_shapes=[
            pltpu.VMEM((WIN, CR, FRONT * CR), F32),
            pltpu.VMEM((8, CR, CR), F32),
            pltpu.VMEM((OUTER, CR, CR), F32),
            pltpu.VMEM((ROWS, CR), F32),
            pltpu.VMEM((ROWS, CR), F32),
            pltpu.VMEM((FRONT, CR, FRONT * CR), F32),
            pltpu.VMEM((FRONT, CR, CR), F32),
            pltpu.SemaphoreType.DMA((8,)),
        ],
        compiler_params=pltpu.CompilerParams(vmem_limit_bytes=60 * 2**20),
        name="front",
    )(owners, front_first, owned, outer.reshape(OUTER, CR, CR), mine, stack, inverse, across_me)


def solution(mesh):
    in_specs = (
        P(("pts", "grp"), None, None, None, None),
        P(("pts", "grp"), None, None),
        P(("pts", "grp"), None, None),
        P(("pts", "grp"), None),
        P(),
        P(("pts", "grp"), None),
        P(),
        P(),
    )
    out_specs = (P(("pts", "grp"), None, None), P(("pts", "grp"), None), P(None, "grp"))
    return jax.shard_map(per_device, mesh=mesh, in_specs=in_specs, out_specs=out_specs, check_vma=False)
```

time: 138 us -> 119 us (0.86)
  Pallas kernels: 132 us -> 116 us
  local copies, waits for them, and re-layouts: 3.74 us -> 0 us
    pallas_call x1, Pallas kernels: 121 us -> 107 us  [per_device(): pl.pallas_call(exchange_kernel, out_shape=(shape(8, CR, CR), shape(OUTER,...]
    pallas_call x1 -> x0, Pallas kernels: 4.48 us -> none  [per_device(): pl.pallas_call(pair_kernel, out_shape=(shape(TILES + 1, CR, CR), shape(RO...]
    unnamed x11 -> x0, local copies, waits for them, and re-layouts: 3.13 us -> none
    pallas_call x1, Pallas kernels: 6.47 us -> 8.82 us  [per_device(): pl.pallas_call(front_kernel, out_shape=(shape(8, CR, CR), shape(1, CR), s...]
where the time goes in v3:
time: 119 us; the launch traced here: 118 us
  Pallas kernels  116 us (97%)
  between operations  1.47 us (1%)
  other arithmetic  1.33 us (1%)
    pallas_call x1, Pallas kernels, per_device(): pl.pallas_call(exchange_kernel, out_shape=(shape(8, CR, CR), shape(OUTER,...  107 us
    pallas_call x1, Pallas kernels, per_device(): pl.pallas_call(front_kernel, out_shape=(shape(8, CR, CR), shape(1, CR), s...  8.82 us

profile of v3, /device:TPU:1, one launch (start us, length us, event | category | flops | bytes accessed | tf_op | source)
XLA Modules:
  0.0 118.3 jit_solution(117486731395359555)
XLA Ops:
  1.3 1.3 %select_reduce_fusion.owners = s32[128]{0:T(128)} fusion(s32[128]{0:T(128)} %param.14), kind=kLoop, calls=%fused_computation | loop fusion | flops 49024 | bytes 1024 | tf_op jit(solution)/shard_map/reduce_sum | solution.py:743
  2.6 106.7 %exchange.1 = (f32[8,128,128]{2,1,0:T(8,128)}, f32[44,2,4,2,8,128]{5,4,3,2,1,0:T(8,128)}, f32[8,128]{1,0:T(8,128)}, f32[8,128]{1,0:T(8,128)}, f32[4,128,512]{2,1,0:T(8,128)}, /*index=5*/f32[4,128,128]{2,1,0:T(8,128)}) custom-call(s32[128]{0:T(128)} %select_reduce_fusion.owners, s32[1]{0:T(128)S(6)} %copy.11.first, s32[1,6]{1,0:T(1,128)} %inc_hbm.1, ...), custom_call_target="tpu_custom_call" | custom-call | tf_op jit(solution)/shard_map/exchange/pallas_call | solution.py:744
  109.3 8.8 %front.1 = (f32[8,128,128]{2,1,0:T(8,128)}, f32[1,128]{1,0:T(1,128)}, f32[2304,128]{1,0:T(8,128)}) custom-call(s32[128]{0:T(128)} %select_reduce_fusion.owners, s32[1]{0:T(128)S(6)} %copy.11.first, f32[8,128,128]{2,1,0:T(8,128)} %get-tuple-element.9.owned_hbm, f32[44,128,128]{2,1,0:T(8,128)} %bitcast.6, f32[8,128]{1,0:T(8,128)} %get-tuple-element.11.mine_hbm, ...), custom_call_target="tpu_custom_call" | custom-call | tf_op jit(solution)/shard_map/front/pallas_call | solution.py:801

commit v4 on v3

--- a/solution.py
+++ b/solution.py
@@ -494,7 +494,7 @@
     def at(j):
         return slice(CR * j, CR * (j + 1))
 
-    hooks = [{8: phase_one}, {8: phase_two}, {8: phase_three}, {}]
+    hooks = [{10: phase_one}, {12: phase_two}, {}, {4: phase_three}]
     for k in range(FRONT):
         factor_rows(square[k, k], upper.at[2 * k], upper.at[2 * k + 1], hooks[k])
         own = upper[2 * k + 1]
@@ -576,32 +576,52 @@
     def down(value, row):
         return jnp.broadcast_to(value[row : row + 1], (ROWS, CR))
 
+    cols = [across(left[0], k) for k in range(ROWS)]
     for b in range(count):
         if b in hooks:
             hooks[b]()
         base = ROWS * b
-        cols = [across(left[b], base + k) for k in range(ROWS)]
+        last = b == count - 1
         e = [[down(cols[j], i) if j <= i else None for j in range(ROWS)] for i in range(ROWS)]
         x = [down(left[b], i) for i in range(ROWS)]
         y = [down(right[b], i) for i in range(ROWS)]
+        if not last:
+            near = [across(left[b + 1], base + k) for k in range(ROWS)]
+            cols = [across(left[b + 1], base + ROWS + k) for k in range(ROWS)]
         inv = []
-        for j in range(ROWS):
-            scale = lax.rsqrt(e[j][j])
-            inv.append(scale)
-            for i in range(j + 1, ROWS):
-                e[i][j] = e[i][j] * scale
-            x[j] = x[j] * scale
-            y[j] = y[j] * scale
-            for i in range(j + 1, ROWS):
-                for k in range(j + 1, i + 1):
-                    e[i][k] = e[i][k] - e[i][j] * e[k][j]
-                x[i] = x[i] - e[i][j] * x[j]
-                y[i] = y[i] - e[i][j] * y[j]
+        for j in range(0, ROWS, 2):
+            p, q, r = e[j][j], e[j + 1][j], e[j + 1][j + 1]
+            one = lax.rsqrt(p)
+            two = one * lax.rsqrt(p * r - q * q)
+            inv += [one, p * two]
+            e[j + 1][j] = q * one
+
+            def pair(u, v):
+                return u * one, (p * v - q * u) * two
+
+            for i in range(j + 2, ROWS):
+                e[i][j], e[i][j + 1] = pair(e[i][j], e[i][j + 1])
+            for i in range(j + 2, ROWS):
+                for k in range(j + 2, i + 1):
+                    e[i][k] = e[i][k] - (e[i][j] * e[k][j] + e[i][j + 1] * e[k][j + 1])
+            x[j], x[j + 1] = pair(x[j], x[j + 1])
+            y[j], y[j + 1] = pair(y[j], y[j + 1])
+            for i in range(j + 2, ROWS):
+                x[i] = x[i] - (e[i][j] * x[j] + e[i][j + 1] * x[j + 1])
+                y[i] = y[i] - (e[i][j] * y[j] + e[i][j + 1] * y[j + 1])
+            if not last:
+                m, n = pair(near[j], near[j + 1])
+                for k in range(j + 2, ROWS):
+                    near[k] = near[k] - (m * e[k][j] + n * e[k][j + 1])
+                for k in range(ROWS):
+                    cols[k] = cols[k] - (m * down(m, k) + n * down(n, k))
+                left[b + 1] = left[b + 1] - (m * x[j] + n * x[j + 1])
+                right[b + 1] = right[b + 1] - (m * y[j] + n * y[j + 1])
         for j in range(ROWS):
             out_upper[base + j : base + j + 1] = x[j][0:1]
             out_inverse[base + j : base + j + 1] = y[j][0:1]
-        if b == count - 1:
-            break
+        if b >= count - 2:
+            continue
         xs = [None] * ROWS
         ys = [None] * ROWS
         for j in reversed(range(ROWS)):
@@ -611,7 +631,7 @@
                 py = py - e[i][j] * ys[i]
             xs[j] = px * inv[j]
             ys[j] = py * inv[j]
-        for s in range(b + 1, count):
+        for s in range(b + 2, count):
             ratios = [across(left[s], base + k) for k in range(ROWS)]
             for k in range(ROWS):
                 left[s] = left[s] - ratios[k] * xs[k]

time: 119 us -> 114 us (0.958)
  Pallas kernels: 116 us -> 110 us
    pallas_call x1, Pallas kernels: 107 us -> 102 us  [per_device(): pl.pallas_call(exchange_kernel, out_shape=(shape(8, CR, CR), shape(OUTER,...]
    pallas_call x1, Pallas kernels: 8.82 us -> 7.18 us  [per_device(): pl.pallas_call(front_kernel, out_shape=(shape(8, CR, CR), shape(1, CR), s...]
where the time goes in v4:
time: 114 us; the launch traced here: 112 us
  Pallas kernels  110 us (96%)
  between operations  1.47 us (1%)
  other arithmetic  1.33 us (1%)
    pallas_call x1, Pallas kernels, per_device(): pl.pallas_call(exchange_kernel, out_shape=(shape(8, CR, CR), shape(OUTER,...  102 us
    pallas_call x1, Pallas kernels, per_device(): pl.pallas_call(front_kernel, out_shape=(shape(8, CR, CR), shape(1, CR), s...  7.18 us

profile of v4, /device:TPU:1, one launch (start us, length us, event | category | flops | bytes accessed | tf_op | source)
XLA Modules:
  0.0 112.4 jit_solution(17859541201953449024)
XLA Ops:
  1.3 1.3 %select_reduce_fusion.owners = s32[128]{0:T(128)} fusion(s32[128]{0:T(128)} %param.14), kind=kLoop, calls=%fused_computation | loop fusion | flops 49024 | bytes 1024 | tf_op jit(solution)/shard_map/reduce_sum | solution.py:763
  2.6 102.4 %exchange.1 = (f32[8,128,128]{2,1,0:T(8,128)}, f32[44,2,4,2,8,128]{5,4,3,2,1,0:T(8,128)}, f32[8,128]{1,0:T(8,128)}, f32[8,128]{1,0:T(8,128)}, f32[4,128,512]{2,1,0:T(8,128)}, /*index=5*/f32[4,128,128]{2,1,0:T(8,128)}) custom-call(s32[128]{0:T(128)} %select_reduce_fusion.owners, s32[1]{0:T(128)S(6)} %copy.11.first, s32[1,6]{1,0:T(1,128)} %inc_hbm.1, ...), custom_call_target="tpu_custom_call" | custom-call | tf_op jit(solution)/shard_map/exchange/pallas_call | solution.py:764
  105.0 7.2 %front.1 = (f32[8,128,128]{2,1,0:T(8,128)}, f32[1,128]{1,0:T(1,128)}, f32[2304,128]{1,0:T(8,128)}) custom-call(s32[128]{0:T(128)} %select_reduce_fusion.owners, s32[1]{0:T(128)S(6)} %copy.11.first, f32[8,128,128]{2,1,0:T(8,128)} %get-tuple-element.9.owned_hbm, f32[44,128,128]{2,1,0:T(8,128)} %bitcast.6, f32[8,128]{1,0:T(8,128)} %get-tuple-element.11.mine_hbm, ...), custom_call_target="tpu_custom_call" | custom-call | tf_op jit(solution)/shard_map/front/pallas_call | solution.py:821
